TPU v7x, 128 devices: a whole 4x4x4 slice. The times are simulated.
128 devices in a mesh: dp: 8 (over x, z_lo), tensor: 16 (over y, z_hi, core).
Axes of the slice: x: 4, y: 4, z: 4 (z_hi: 2, z_lo: 2; z = z_hi * 2 + z_lo), core: 2. Of those that a mesh axis runs over, the one named last changes fastest.
Arguments:
- tokens: bfloat16 [1024, 8192], P('dp', 'tensor'), may hold values from -6 to 6
- gate_weight: bfloat16 [8192, 16384], P(('dp', 'tensor')), may hold values from -0.0625 to 0.0625
- up_weight: bfloat16 [8192, 16384], P(('dp', 'tensor')), may hold values from -0.0625 to 0.0625
- gate_tangent: bfloat16 [8192, 16384], P(('dp', 'tensor')), may hold values from -0.0625 to 0.0625
- up_tangent: bfloat16 [8192, 16384], P(('dp', 'tensor')), may hold values from -0.0625 to 0.0625
- adjoint: bfloat16 [1024, 16384], P(None, ('dp', 'tensor')), may hold values from -0.1875 to 0.1875
Outputs:
- hvp_gate: float32 [8192, 16384], P(None, ('dp', 'tensor'))
- hvp_up: float32 [8192, 16384], P(None, ('dp', 'tensor'))
All inputs are finite; a program needn't handle non-finite values.
Results may differ from a plain program's by a relative error of at most 0.0055.
Values may be sent and summed in bfloat16 or wider, within the bound.
A program may use at most 192 MiB of HBM per device.

v0:
```python
import jax
import jax.numpy as jnp
from jax import lax
from jax.sharding import PartitionSpec as P

epsilon = 1e-05


def hidden_terms(forward, adjoint, col_width):
    gate_pre = forward[:, :col_width]
    up_pre = forward[:, col_width : 2 * col_width]
    gate_dot = forward[:, 2 * col_width : 3 * col_width]
    up_dot = forward[:, 3 * col_width :]
    cotangent = adjoint.astype(jnp.float32)
    logistic = jax.nn.sigmoid(gate_pre)
    first = logistic * (1.0 + gate_pre * (1.0 - logistic))
    second = logistic * (1.0 - logistic) * (2.0 + gate_pre * (1.0 - 2.0 * logistic))
    gate_term = (cotangent * (up_dot * first + up_pre * second * gate_dot)).astype(jnp.bfloat16)
    up_term = (cotangent * first * gate_dot).astype(jnp.bfloat16)
    return jnp.concatenate([gate_term, up_term], axis=1)


def token_product(normed_rows, terms):
    return lax.dot_general(
        normed_rows, terms, (((0,), (0,)), ((), ())), preferred_element_type=jnp.float32
    )


def local(tokens, gate_weight, up_weight, gate_tangent, up_tangent, adjoint):
    local_rows = gate_weight.shape[0]
    dp_count = lax.axis_size("dp")
    tp_count = lax.axis_size("tensor")
    all_count = dp_count * tp_count
    col_width = gate_weight.shape[1] // all_count
    stacked = jnp.concatenate(
        [
            matrix.reshape(local_rows, all_count, col_width)
            for matrix in (gate_weight, up_weight, gate_tangent, up_tangent)
        ],
        axis=2,
    )
    moved = lax.all_to_all(stacked, ("dp", "tensor"), split_axis=1, concat_axis=0, tiled=True)
    columns = moved.reshape(local_rows * all_count, 4 * col_width)
    features = lax.all_gather(tokens, "tensor", axis=1, tiled=True)
    wide = features.astype(jnp.float32)
    variance = jnp.mean(wide * wide, axis=1, keepdims=True) + epsilon
    normed = (wide * lax.rsqrt(variance)).astype(jnp.bfloat16)
    every_row = lax.all_gather(normed, "dp", axis=0, tiled=True)
    forward = jnp.dot(every_row, columns, preferred_element_type=jnp.float32)
    terms = hidden_terms(forward, adjoint, col_width)
    product = token_product(every_row, terms)
    return (product[:, :col_width], product[:, col_width:])


def solution(mesh):
    in_specs = (
        P("dp", "tensor"),
        P(("dp", "tensor"), None),
        P(("dp", "tensor"), None),
        P(("dp", "tensor"), None),
        P(("dp", "tensor"), None),
        P(None, ("dp", "tensor")),
    )
    out_specs = (P(None, ("dp", "tensor")), P(None, ("dp", "tensor")))
    return jax.shard_map(local, mesh=mesh, in_specs=in_specs, out_specs=out_specs, check_vma=False)
```

profile of v0, /device:TPU:12, one launch (start us, length us, event | category | flops | bytes accessed | tf_op | source)
XLA Modules:
  0.0 534.8 jit_solution(8374899834970744060)
XLA Ops:
  7.2 0.0 all-gather.3.cloned.1.call-start
  7.2 0.7 all-gather.3.cloned.1.call-update
  7.9 0.0 copy-start
  7.9 0.0 all-gather.5.cloned.1.call-start
  8.0 54.0 %all-gather.3.cloned.1.call-done = bf16[128,8192]{1,0:T(8,128)(2,1)} async-done(((bf16[128,512]{1,0:T(8,128)(2,1)}), bf16[128,8192]{1,0:T(8,128)(2,1)}) %all-gather.3.cloned.1.call-update) | async-done | bytes 2097168 | tf_op jit(solution)/shard_map/all_gather | solution.py:44
  62.0 2.1 fusion
  64.0 3.4 fusion.1
  67.4 0.0 all-gather.5.cloned.1.call-update
  67.4 0.0 copy-start.1
  67.4 0.0 copy-done
  67.4 0.0 copy-start.2
  67.5 0.6 copy.16
  68.0 1.0 copy-done.1
  69.0 0.0 copy-start.3
  69.0 0.6 copy.17
  69.6 0.1 copy-done.2
  69.7 0.6 copy.14
  70.2 0.5 copy-done.3
  70.8 0.6 copy.15
  71.3 3.9 pad_maximum_fusion
  75.2 11.8 %copy.13 = bf16[64,128,512]{2,0,1:T(8,128)(2,1)} copy(bf16[64,128,512]{2,1,0:T(8,128)(2,1)} %pad_maximum_fusion) | data formatting | bytes 16777216 | tf_op jit(solution)/shard_map/concatenate | solution.py:35
  87.1 0.0 copy-start.4
  87.1 7.4 %all-to-all-start = ((bf16[64,128,512]{2,0,1:T(8,128)(2,1)}), bf16[64,128,512]{2,0,1:T(8,128)(2,1)}, u32[]{:S(2)}, u32[]{:S(2)}) async-start(bf16[64,128,512]{2,0,1:T(8,128)(2,1)} %copy.13), calls=%async_computation | async-start | bytes 16777216 | tf_op jit(solution)/shard_map/all_to_all | solution.py:42
  94.5 0.0 copy-done.4
  94.5 0.1 copy.12
  94.6 115.1 %all-to-all-done = bf16[64,128,512]{2,0,1:T(8,128)(2,1)} async-done(((bf16[64,128,512]{2,0,1:T(8,128)(2,1)}), bf16[64,128,512]{2,0,1:T(8,128)(2,1)}, u32[]{:S(2)}, u32[]{:S(2)}) %all-to-all-start) | async-done | bytes 8388640 | tf_op jit(solution)/shard_map/all_to_all | solution.py:42
  209.7 288.1 %all-gather.5.cloned.1.call-done = bf16[1024,8192]{1,0:T(8,128)(2,1)} async-done(((bf16[128,8192]{1,0:T(8,128)(2,1)}), bf16[1024,8192]{1,0:T(8,128)(2,1)}) %all-gather.5.cloned.1.call-update) | async-done | bytes 16777232 | tf_op jit(solution)/shard_map/all_gather | solution.py:48
  497.8 17.2 %fusion.17 = f32[1024,512]{0,1:T(8,128)S(1)} fusion(bf16[1024,8192]{1,0:T(8,128)(2,1)} %all-gather.5.cloned.1.call-done, bf16[8192,512]{1,0:T(8,128)(2,1)} %bitcast.2), kind=kOutput, calls=%fused_computation.27 | convolution fusion | flops 8589934592 | bytes 27262976 | tf_op jit(solution)/shard_map/dot_general | solution.py:49
  515.1 0.4 fusion.2
  515.5 8.5 %fusion.11 = f32[8192,256]{1,0:T(8,128)S(1)} fusion(bf16[1024,8192]{1,0:T(8,128)(2,1)} %all-gather.5.cloned.1.call-done, bf16[1024,128]{0,1:T(8,128)(2,1)S(1)} %get-tuple-element.5, bf16[1024,128]{0,1:T(8,128)(2,1)S(1)} %get-tuple-element.4), kind=kOutput, calls=%fused_computation.19 | convolution fusion | flops 4296015872 | bytes 25690112 | tf_op jit(solution)/shard_map/dot_general | solution.py:24
  524.0 3.9 fusion.16
  (1 shorter events, 0.0 us)
Async XLA Ops:
  7.2 54.8 %all-gather.3.cloned.1.call-start = ((), (), s32[]{:S(2)}) async-start(), calls=%async_computation.1 | async-start | bytes 2228224 | tf_op jit(solution)/shard_map/all_gather | solution.py:44
  7.9 59.5 %copy-start = (bf16[64,16384]{1,0:T(8,128)(2,1)S(1)}, bf16[64,16384]{1,0:T(8,128)(2,1)}, u32[]{:S(2)}) copy-start(bf16[64,16384]{1,0:T(8,128)(2,1)} %param.9) | copy-start | bytes 6291460
  7.9 489.9 %all-gather.5.cloned.1.call-start = ((), (), s32[]{:S(2)}) async-start(), calls=%async_computation.2 | async-start | bytes 18874368 | tf_op jit(solution)/shard_map/all_gather | solution.py:48
  67.4 1.6 copy-start.1
  67.4 2.2 copy-start.2
  69.0 1.7 copy-start.3
  87.1 7.4 %copy-start.4 = (bf16[1024,128]{1,0:T(8,128)(2,1)S(1)}, bf16[1024,128]{1,0:T(8,128)(2,1)}, u32[]{:S(2)}) copy-start(bf16[1024,128]{1,0:T(8,128)(2,1)} %param.11) | copy-start | bytes 786436
  87.1 122.7 %all-to-all-start = ((bf16[64,128,512]{2,0,1:T(8,128)(2,1)}), bf16[64,128,512]{2,0,1:T(8,128)(2,1)}, u32[]{:S(2)}, u32[]{:S(2)}) async-start(bf16[64,128,512]{2,0,1:T(8,128)(2,1)} %copy.13), calls=%async_computation | async-start | bytes 16777216 | tf_op jit(solution)/shard_map/all_to_all | solution.py:42
Sparse Core Ops, SparseCore 0:
  10.3 51.6 all-gather.2
  67.5 430.2 all-gather.4
where the time goes:
time: 535 us
  waiting for transfers between devices  458 us (86%)
  matrix products  25.8 us (5%)
  local copies, waits for them, and re-layouts  19.8 us (4%)
  between operations  14.2 us (3%)
  other arithmetic  9.77 us (2%)
  starting transfers between devices  7.48 us (1%)
    all_gather x1, waiting for transfers between devices, local(): every_row = lax.all_gather(normed, 'dp', axis=0, tiled=True)  288 us
    all_to_all x1, waiting for transfers between devices, local(): lax.all_to_all(stacked, ('dp', 'tensor'), split_axis=1, concat_axis=0, ti...  115 us
    all_gather x1, waiting for transfers between devices, local(): features = lax.all_gather(tokens, 'tensor', axis=1, tiled=True)  54 us
    dot_general x1, matrix products, local(): forward = jnp.dot(every_row, columns, preferred_element_type=jnp.float32)  17.2 us
    concatenate x1, local copies, waits for them, and re-layouts, local(): jnp.concatenate([matrix.reshape(local_rows, all_count, col_width) for mat...  11.8 us
  transfers between devices with their start and end apart: 3, of which 3 were waited for; matrix products, arithmetic and copies ran while one was open for 3% of the time, Pallas kernels for 0%

commit v1 on v0

v1 whole, which is shorter than its diff:
```python
import jax
import jax.numpy as jnp
from jax import lax
from jax.experimental import pallas as pl
from jax.experimental.pallas import tpu as pltpu
from jax.sharding import PartitionSpec as P

epsilon = 1e-05
MESH = pl.DeviceIdType.MESH
BF16, F32 = jnp.bfloat16, jnp.float32
PLANE = (
    (1, 0), (0, 1), (3, 0), (0, 3), (2, 0), (0, 2), (1, 1), (3, 3),
    (1, 3), (3, 1), (1, 2), (2, 1), (3, 2), (2, 3), (2, 2),
)
WAVES = (2, 1, 3, 0)


def place():
    dp, t = lax.axis_index("dp"), lax.axis_index("tensor")
    return dp // 2, t // 4, ((t // 2) % 2) * 2 + dp % 2, t % 2


def device(x, y, z, c):
    return (x * 2 + z % 2, (y * 2 + z // 2) * 2 + c)


def chip_in_plane(y, z):
    return (z % 2) * 8 + y * 2 + z // 2


def hidden_terms(forward, adjoint):
    gate_pre, up_pre = forward[:, :128], forward[:, 128:256]
    gate_dot, up_dot = forward[:, 256:384], forward[:, 384:]
    cotangent = adjoint.astype(F32)
    logistic = jax.nn.sigmoid(gate_pre)
    first = logistic * (1.0 + gate_pre * (1.0 - logistic))
    second = logistic * (1.0 - logistic) * (2.0 + gate_pre * (1.0 - 2.0 * logistic))
    gate_term = (cotangent * (up_dot * first + up_pre * second * gate_dot)).astype(BF16)
    up_term = (cotangent * first * gate_dot).astype(BF16)
    return gate_term, up_term


def exchange(
    tokens, adjoint, w0, w1, w2, w3, gathered, terms,
    staged, theirs, packed, arrived, stats, own, slab_t, slab, sums, sent, got,
    stage_sem, their_send, their_recv, wave_send, wave_recv, stat_sem, local_sem,
    y_sem, z_sem, x_send, x_left, x_right, f_send, f_left, f_right, d_send, d_recv, p_send, p_recv,
):
    weights = (w0, w1, w2, w3)
    x, y, z, c = place()
    me = chip_in_plane(y, z)
    right, left, across = (x + 1) % 4, (x + 3) % 4, (x + 2) % 4
    partner = device(x, y, z, 1 - c)

    def stage_copies(w):
        start = pl.multiple_of(((x + WAVES[w]) % 4) * 4096, 4096)
        return [
            pltpu.make_async_copy(
                weights[m].at[:, pl.ds(start, 4096)], staged.at[w % 2, m], stage_sem.at[w % 2, m]
            )
            for m in range(4)
        ]

    def stage(w):
        for copy in stage_copies(w):
            copy.start()

    def their_copy(w):
        return pltpu.make_async_remote_copy(
            theirs.at[w % 2],
            packed.at[w, :, :, pl.ds(pl.multiple_of(c * 64, 64), 64), :],
            their_send.at[w % 2],
            their_recv.at[w],
            partner,
            MESH,
        )

    def pack(w):
        for copy in stage_copies(w):
            copy.wait()
        if w >= 2:
            their_copy(w - 2).wait_send()

        @pl.loop(0, 16)
        def _(q):
            for m in range(4):
                both = staged[w % 2, m, :, pl.ds(pl.multiple_of(q * 256, 256), 256)]
                low, high = both[:, :128], both[:, 128:]
                packed[w, q, m, pl.ds(pl.multiple_of(c * 64, 64), 64), :] = jnp.where(c == 0, low, high)
                theirs[w % 2, q, m] = jnp.where(c == 0, high, low)

        their_copy(w).start()
        if w + 2 < 4:
            stage(w + 2)

    def send_wave(w):
        their_copy(w).wait_recv()
        for dy, dz in PLANE:
            to_y, to_z = (y + dy) % 4, (z + dz) % 4
            pltpu.make_async_remote_copy(
                packed.at[w, chip_in_plane(to_y, to_z)],
                arrived.at[w, me],
                wave_send.at[w],
                wave_recv.at[w],
                device(x, to_y, to_z, c),
                MESH,
            ).start()
        pltpu.make_async_copy(packed.at[w, me], arrived.at[w, me], wave_recv.at[w]).start()

    def wait_bytes(ref, sem):
        pltpu.make_async_copy(ref, ref, sem).wait()

    def partial_copy(w):
        return pltpu.make_async_remote_copy(
            sent.at[w], got.at[w], p_send.at[w], p_recv.at[w],
            device((x + WAVES[w]) % 4, y, z, c), MESH,
        )

    def share(block, which):
        pltpu.make_async_remote_copy(block, block, d_send, d_recv.at[which], partner, MESH).start()

    to_right, to_left = device(right, y, z, c), device(left, y, z, c)
    right_order = [(x + 2) % 4, (x + 1) % 4, (x + 3) % 4, x]
    left_order = [(x + 2) % 4, (x + 3) % 4, (x + 1) % 4, x]

    def send_group(i):
        block = gathered.at[x, right_order[i], c]
        pltpu.make_async_remote_copy(block, block, x_send, x_left.at[i], to_right, MESH).start()
        block = gathered.at[x, left_order[i], c]
        pltpu.make_async_remote_copy(block, block, x_send, x_right.at[i], to_left, MESH).start()

    from_left = [(x + 1) % 4, x, (x + 2) % 4, (x + 3) % 4]
    from_right = [(x + 3) % 4, x, (x + 2) % 4, (x + 1) % 4]

    def pass_on(i):
        wait_bytes(gathered.at[left, from_left[i], c], x_left.at[i])
        half = gathered.at[left, from_left[i], c, pl.ds(0, 2)]
        pltpu.make_async_remote_copy(half, half, f_send, f_left.at[i], to_right, MESH).start()
        wait_bytes(gathered.at[right, from_right[i], c], x_right.at[i])
        half = gathered.at[right, from_right[i], c, pl.ds(2, 2)]
        pltpu.make_async_remote_copy(half, half, f_send, f_right.at[i], to_left, MESH).start()
        share(gathered.at[left, from_left[i], c], 0 if i == 1 else 1)
        share(gathered.at[right, from_right[i], c], 0 if i == 1 else 1)

    across_left = [x, (x + 3) % 4, (x + 1) % 4, (x + 2) % 4]
    across_right = [x, (x + 1) % 4, (x + 3) % 4, (x + 2) % 4]

    def take_across(i):
        half = gathered.at[across, across_left[i], c, pl.ds(0, 2)]
        wait_bytes(half, f_left.at[i])
        share(half, 0 if i == 0 else 1)
        half = gathered.at[across, across_right[i], c, pl.ds(2, 2)]
        wait_bytes(half, f_right.at[i])
        share(half, 0 if i == 0 else 1)

    def forward(w):
        wait_bytes(arrived.at[w], wave_recv.at[w])
        if w + 2 < 4:
            send_wave(w + 2)

        @pl.loop(0, 2)
        def _(half):
            rows = pl.ds(pl.multiple_of(half * 512, 512), 512)
            lhs = jnp.concatenate([slab[k, rows, :] for k in range(4)], axis=1)
            rhs = jnp.concatenate([arrived[w, :, m].reshape(2048, 128) for m in range(4)], axis=1)
            total = jnp.dot(lhs, rhs, preferred_element_type=F32)
            if w < 3:
                sent[w, rows, :] = total.astype(BF16)
            else:
                sums[rows, :] = total

        if w < 3:
            partial_copy(w).start()

    stage(0)
    stage(1)
    barrier = pltpu.get_barrier_semaphore()
    peers = [device(x, (y + dy) % 4, (z + dz) % 4, c) for dy, dz in PLANE]
    stat_peers = [
        device(x, (y + dy) % 4, (z + dz) % 4, (c + dc) % 2)
        for dy in range(4) for dz in (0, 2) for dc in range(2) if dy or dz or dc
    ]
    cross_peers = [
        device(x, (y + dy) % 4, (z + dz) % 4, 1 - c) for dy in range(4) for dz in (0, 2)
    ]
    x_peers = [device((x + d) % 4, y, z, c) for d in (1, 2, 3)]
    everyone = peers + cross_peers + x_peers
    for peer in everyone:
        pl.semaphore_signal(barrier, 1, device_id=peer, device_id_type=MESH)

    wide = jnp.transpose(tokens[...].astype(F32))
    t = lax.axis_index("tensor")
    stats[t] = jnp.broadcast_to(jnp.sum(wide * wide, axis=0, keepdims=True), (8, 128))
    pl.semaphore_wait(barrier, len(everyone))
    for peer in stat_peers:
        pltpu.make_async_remote_copy(
            stats.at[t], stats.at[t], stat_sem.at[0], stat_sem.at[1], peer, MESH
        ).start()
    pack(0)
    wait_bytes(stats.at[pl.ds(0, 15)], stat_sem.at[1])
    total = stats[0]
    for i in range(1, 16):
        total = total + stats[i]
    scale = lax.rsqrt(total[:1] * (1.0 / 8192.0) + epsilon)
    wide = jnp.transpose(tokens[...].astype(F32))
    own[...] = (wide * scale).astype(BF16)
    mine = gathered.at[x, y, c, z]
    for d in (1, 3, 2):
        pltpu.make_async_remote_copy(
            own, mine, y_sem.at[0], y_sem.at[1], device(x, (y + d) % 4, z, c), MESH
        ).start()
    local = pltpu.make_async_copy(own, mine, local_sem)
    local.start()
    send_wave(0)
    pack(1)
    local.wait()
    wait_bytes(gathered.at[x, pl.ds(0, 3), c, z], y_sem.at[1])
    column = gathered.at[x, :, c, z]
    for d in (1, 3, 2):
        pltpu.make_async_remote_copy(
            column, column, z_sem.at[0], z_sem.at[1], device(x, y, (z + d) % 4, c), MESH
        ).start()
    send_wave(1)
    pack(2)
    wait_bytes(gathered.at[x, pl.ds(0, 3), c], z_sem.at[1])
    send_group(0)
    send_group(1)
    share(gathered.at[x, x, c], 0)
    for d in (1, 2, 3):
        share(gathered.at[x, (x + d) % 4, c], 1)
    pack(3)
    pass_on(0)
    send_group(2)
    pass_on(1)
    send_group(3)
    take_across(0)
    wait_bytes(gathered.at[:, x, 1 - c], d_recv.at[0])
    load = pltpu.make_async_copy(gathered.at[:, x], slab_t, local_sem)
    load.start()
    load.wait()

    @pl.loop(0, 4)
    def _(from_x):
        for from_c in range(2):
            for from_z in range(4):
                dp = from_x * 2 + from_z % 2
                rows = pl.ds(pl.multiple_of(dp * 128, 128), 128)
                slab[(from_z // 2) * 2 + from_c, rows, :] = jnp.transpose(slab_t[from_x, from_c, from_z])

    forward(0)
    pass_on(2)
    forward(1)
    pass_on(3)
    take_across(1)
    forward(2)
    take_across(2)
    take_across(3)
    forward(3)
    for w in range(3):
        partial_copy(w).wait_recv()

    @pl.loop(0, 4)
    def _(part):
        rows = pl.ds(pl.multiple_of(part * 256, 256), 256)
        total = sums[rows, :]
        for w in range(3):
            total = total + got[w, rows, :].astype(F32)
        gate_term, up_term = hidden_terms(total, adjoint[rows, :])
        terms[rows, :128] = gate_term
        terms[rows, 128:] = up_term

    wait_bytes(gathered.at[pl.ds(0, 3), pl.ds(0, 2)], d_recv.at[1])
    for w in range(3):
        partial_copy(w).wait_send()
    for w in range(4):
        wait_bytes(packed.at[w, pl.ds(0, 15)], wave_send.at[w])
    for w in (2, 3):
        their_copy(w).wait_send()
    wait_bytes(stats.at[pl.ds(0, 15)], stat_sem.at[0])
    wait_bytes(gathered.at[0, 0, 0, pl.ds(0, 3)], y_sem.at[0])
    wait_bytes(gathered.at[0, pl.ds(0, 3), 0], z_sem.at[0])
    wait_bytes(gathered.at[0], x_send)
    wait_bytes(gathered.at[0, pl.ds(0, 2)], f_send)
    wait_bytes(gathered.at[pl.ds(0, 2)], d_send)


def product(blocks, terms, gate, up):
    lhs = jnp.concatenate([blocks[i, 0, 0, j] for i in range(4) for j in range(2)], axis=1)
    result = jnp.dot(lhs, terms[...], preferred_element_type=F32)
    gate[...] = result[:, :128]
    up[...] = result[:, 128:]


def local(tokens, gate_weight, up_weight, gate_tangent, up_tangent, adjoint):
    dma = pltpu.SemaphoreType.DMA
    gathered, terms = pl.pallas_call(
        exchange,
        out_shape=(
            jax.ShapeDtypeStruct((4, 4, 2, 4, 512, 128), BF16),
            jax.ShapeDtypeStruct((1024, 256), BF16),
        ),
        in_specs=[pl.BlockSpec(memory_space=pltpu.VMEM)] * 2 + [pl.BlockSpec(memory_space=pl.ANY)] * 4,
        out_specs=(pl.BlockSpec(memory_space=pl.ANY), pl.BlockSpec(memory_space=pltpu.VMEM)),
        scratch_shapes=[
            pltpu.VMEM((2, 4, 64, 4096), BF16),
            pltpu.VMEM((2, 16, 4, 64, 128), BF16),
            pltpu.VMEM((4, 16, 4, 128, 128), BF16),
            pltpu.VMEM((4, 16, 4, 128, 128), BF16),
            pltpu.VMEM((16, 8, 128), F32),
            pltpu.VMEM((512, 128), BF16),
            pltpu.VMEM((4, 2, 4, 512, 128), BF16),
            pltpu.VMEM((4, 1024, 512), BF16),
            pltpu.VMEM((1024, 512), F32),
            pltpu.VMEM((3, 1024, 512), BF16),
            pltpu.VMEM((3, 1024, 512), BF16),
            dma((2, 4)), dma((2,)), dma((4,)), dma((4,)), dma((4,)), dma((2,)), dma,
            dma((2,)), dma((2,)), dma, dma((4,)), dma((4,)), dma, dma((4,)), dma((4,)),
            dma, dma((2,)), dma((3,)), dma((3,)),
        ],
        compiler_params=pltpu.CompilerParams(
            collective_id=0, has_side_effects=True, vmem_limit_bytes=58 * 2**20
        ),
        name="exchange",
    )(tokens, adjoint, gate_weight, up_weight, gate_tangent, up_tangent)

    return pl.pallas_call(
        product,
        grid=(16,),
        out_shape=(jax.ShapeDtypeStruct((8192, 128), F32),) * 2,
        in_specs=[
            pl.BlockSpec((4, 1, 1, 2, 512, 128), lambda t: (0, t // 4, t % 2, (t // 2) % 2, 0, 0)),
            pl.BlockSpec((1024, 256), lambda t: (0, 0)),
        ],
        out_specs=(pl.BlockSpec((512, 128), lambda t: (t, 0)),) * 2,
        compiler_params=pltpu.CompilerParams(vmem_limit_bytes=58 * 2**20),
        name="product",
    )(gathered, terms)


def solution(mesh):
    in_specs = (
        P("dp", "tensor"),
        P(("dp", "tensor"), None),
        P(("dp", "tensor"), None),
        P(("dp", "tensor"), None),
        P(("dp", "tensor"), None),
        P(None, ("dp", "tensor")),
    )
    out_specs = (P(None, ("dp", "tensor")), P(None, ("dp", "tensor")))
    return jax.shard_map(local, mesh=mesh, in_specs=in_specs, out_specs=out_specs, check_vma=False)
```

time: 535 us -> 218 us (0.41)
  the two profiles are of different devices: /device:TPU:12 before, /device:TPU:1 now
where the time goes in v1:
time: 218 us; the launch traced here: 217 us
  Pallas kernels  216 us (99%)
    pallas_call x1, Pallas kernels, local(): pl.pallas_call(exchange, out_shape=(jax.ShapeDtypeStruct((4, 4, 2, 4, 512...  200 us
    pallas_call x1, Pallas kernels, local(): pl.pallas_call(product, grid=(16,), out_shape=(jax.ShapeDtypeStruct((8192...  16.8 us

profile of v1, /device:TPU:1, one launch (start us, length us, event | category | flops | bytes accessed | tf_op | source)
XLA Modules:
  0.0 217.0 jit_solution(3855266459533033778)
XLA Ops:
  0.6 199.5 %exchange.1 = (bf16[4,4,2,4,512,128]{5,4,3,2,1,0:T(8,128)(2,1)}, bf16[1024,256]{1,0:T(8,128)(2,1)}) custom-call(bf16[128,512]{1,0:T(8,128)(2,1)} %tokens.1, bf16[1024,128]{1,0:T(8,128)(2,1)} %adjoint.1, bf16[64,16384]{1,0:T(8,128)(2,1)} %w0.1, bf16[64,16384]{1,0:T(8,128)(2,1)} %w1.1, bf16[64,16384]{1,0:T(8,128)(2,1)} %w2.1, bf16[64,16384]{1,0:T(8,128)(2,1)} %w3.1), custom_call_target="tpu_custom_call" | custom-call | tf_op jit(solution)/shard_map/exchange/pallas_call | solution.py:296
  200.1 16.8 %product.1 = (f32[8192,128]{1,0:T(8,128)}, f32[8192,128]{1,0:T(8,128)}) custom-call(bf16[4,4,2,4,512,128]{5,4,3,2,1,0:T(8,128)(2,1)} %get-tuple-element.4.blocks, bf16[1024,256]{1,0:T(8,128)(2,1)} %get-tuple-element.5.terms), custom_call_target="tpu_custom_call" | custom-call | tf_op jit(solution)/shard_map/product/pallas_call | solution.py:326

commit v2 on v1

v2 whole, which is shorter than its diff:
```python
import jax
import jax.numpy as jnp
from jax import lax
from jax.experimental import pallas as pl
from jax.experimental.pallas import tpu as pltpu
from jax.sharding import PartitionSpec as P

epsilon = 1e-05
MESH = pl.DeviceIdType.MESH
BF16, F32 = jnp.bfloat16, jnp.float32
PLANE = (
    (1, 0), (0, 1), (3, 0), (0, 3), (2, 0), (0, 2), (1, 1), (3, 3),
    (1, 3), (3, 1), (1, 2), (2, 1), (3, 2), (2, 3), (2, 2),
)
WAVES = (2, 1, 3, 0)


def place():
    dp, t = lax.axis_index("dp"), lax.axis_index("tensor")
    return dp // 2, t // 4, ((t // 2) % 2) * 2 + dp % 2, t % 2


def device(x, y, z, c):
    return (x * 2 + z % 2, (y * 2 + z // 2) * 2 + c)


def chip_in_plane(y, z):
    return (z % 2) * 8 + y * 2 + z // 2


def hidden_terms(forward, adjoint):
    gate_pre, up_pre = forward[:, :128], forward[:, 128:256]
    gate_dot, up_dot = forward[:, 256:384], forward[:, 384:]
    cotangent = adjoint.astype(F32)
    logistic = jax.nn.sigmoid(gate_pre)
    first = logistic * (1.0 + gate_pre * (1.0 - logistic))
    second = logistic * (1.0 - logistic) * (2.0 + gate_pre * (1.0 - 2.0 * logistic))
    gate_term = (cotangent * (up_dot * first + up_pre * second * gate_dot)).astype(BF16)
    up_term = (cotangent * first * gate_dot).astype(BF16)
    return gate_term, up_term


def exchange(
    tokens, adjoint, w0, w1, w2, w3, gathered, terms,
    staged, theirs, packed, arrived, stats, own, slab_t, slab, sums, held, sent, passing, got,
    stage_sem, their_send, their_recv, wave_send, wave_recv, stat_sem, local_sem,
    a_sem, b_send, b_recv, x_send, x_left, x_right, f_send, f_left, f_right, d_send, d_recv,
    pass_send, pass_recv, p_send, p_recv,
):
    weights = (w0, w1, w2, w3)
    x, y, z, c = place()
    me = chip_in_plane(y, z)
    right, left, across = (x + 1) % 4, (x + 3) % 4, (x + 2) % 4
    partner = device(x, y, z, 1 - c)
    to_right, to_left = device(right, y, z, c), device(left, y, z, c)
    a, b = y * (1 - c) + z * c, z * (1 - c) + y * c

    def at_ab(to_a, to_b):
        return device(x, to_a * (1 - c) + to_b * c, to_b * (1 - c) + to_a * c, c)

    def stage_copies(w):
        start = pl.multiple_of(((x + WAVES[w]) % 4) * 4096, 4096)
        return [
            pltpu.make_async_copy(
                weights[m].at[:, pl.ds(start, 4096)], staged.at[w % 2, m], stage_sem.at[w % 2, m]
            )
            for m in range(4)
        ]

    def stage(w):
        for copy in stage_copies(w):
            copy.start()

    def their_copy(w):
        return pltpu.make_async_remote_copy(
            theirs.at[w % 2],
            packed.at[w, :, :, pl.ds(pl.multiple_of(c * 64, 64), 64), :],
            their_send.at[w % 2],
            their_recv.at[w],
            partner,
            MESH,
        )

    def pack(w):
        for copy in stage_copies(w):
            copy.wait()
        if w >= 2:
            their_copy(w - 2).wait_send()

        @pl.loop(0, 16)
        def _(q):
            for m in range(4):
                both = staged[w % 2, m, :, pl.ds(pl.multiple_of(q * 256, 256), 256)]
                low, high = both[:, :128], both[:, 128:]
                packed[w, q, m, pl.ds(pl.multiple_of(c * 64, 64), 64), :] = jnp.where(c == 0, low, high)
                theirs[w % 2, q, m] = jnp.where(c == 0, high, low)

        their_copy(w).start()
        if w + 2 < 4:
            stage(w + 2)

    def send_wave(w):
        their_copy(w).wait_recv()
        for dy, dz in PLANE:
            to_y, to_z = (y + dy) % 4, (z + dz) % 4
            pltpu.make_async_remote_copy(
                packed.at[w, chip_in_plane(to_y, to_z)],
                arrived.at[w, me],
                wave_send.at[w],
                wave_recv.at[w],
                device(x, to_y, to_z, c),
                MESH,
            ).start()
        pltpu.make_async_copy(packed.at[w, me], arrived.at[w, me], wave_recv.at[w]).start()

    def wait_bytes(ref, sem):
        pltpu.make_async_copy(ref, ref, sem).wait()

    def share(block):
        pltpu.make_async_remote_copy(block, block, d_send, d_recv, partner, MESH).start()

    column_b = [b, (b + 3) % 4, (b + 1) % 4, (b + 2) % 4]

    def send_column(i):
        block = gathered.at[x, :, c, column_b[i]]
        if i > 0:
            wait_bytes(block, b_recv.at[i - 1])
        pltpu.make_async_remote_copy(block, block, x_send, x_left.at[i], to_right, MESH).start()
        pltpu.make_async_remote_copy(block, block, x_send, x_right.at[i], to_left, MESH).start()
        share(block)

    def pass_on(i):
        block = gathered.at[left, :, c, column_b[i]]
        wait_bytes(block, x_left.at[i])
        half = gathered.at[left, pl.ds(0, 2), c, column_b[i]]
        pltpu.make_async_remote_copy(half, half, f_send, f_left.at[i], to_right, MESH).start()
        share(block)
        block = gathered.at[right, :, c, column_b[i]]
        wait_bytes(block, x_right.at[i])
        half = gathered.at[right, pl.ds(2, 2), c, column_b[i]]
        pltpu.make_async_remote_copy(half, half, f_send, f_right.at[i], to_left, MESH).start()
        share(block)

    def take_across(i):
        wait_bytes(gathered.at[across, pl.ds(0, 2), c, column_b[i]], f_left.at[i])
        wait_bytes(gathered.at[across, pl.ds(2, 2), c, column_b[i]], f_right.at[i])
        share(gathered.at[across, :, c, column_b[i]])

    def forward(w, half):
        lhs = jnp.concatenate([slab[k, half * 512 : half * 512 + 512, :] for k in range(4)], axis=1)
        rhs = jnp.concatenate([arrived[w, :, m].reshape(2048, 128) for m in range(4)], axis=1)
        return jnp.dot(lhs, rhs, preferred_element_type=F32)

    def pass_copy(half):
        return pltpu.make_async_remote_copy(
            sent.at[0, half], passing.at[half], pass_send.at[half], pass_recv.at[half],
            to_left if half else to_right, MESH,
        )

    def partial_copy(w, half):
        return pltpu.make_async_remote_copy(
            sent.at[w, half], got.at[w - 1, half], p_send.at[w - 1, half], p_recv.at[w - 1, half],
            to_left if w == 2 else to_right, MESH,
        )

    stage(0)
    stage(1)
    barrier = pltpu.get_barrier_semaphore()
    peers = [device(x, (y + dy) % 4, (z + dz) % 4, c) for dy, dz in PLANE]
    stat_peers = [
        device(x, (y + dy) % 4, (z + dz) % 4, (c + dc) % 2)
        for dy in range(4) for dz in (0, 2) for dc in range(2) if dy or dz or dc
    ]
    cross_peers = [
        device(x, (y + dy) % 4, (z + dz) % 4, 1 - c) for dy in range(4) for dz in (0, 2)
    ]
    everyone = peers + cross_peers + [to_right, to_left]
    for peer in everyone:
        pl.semaphore_signal(barrier, 1, device_id=peer, device_id_type=MESH)

    wide = jnp.transpose(tokens[...].astype(F32))
    t = lax.axis_index("tensor")
    stats[t] = jnp.broadcast_to(jnp.sum(wide * wide, axis=0, keepdims=True), (8, 128))
    pl.semaphore_wait(barrier, len(everyone))
    for peer in stat_peers:
        pltpu.make_async_remote_copy(
            stats.at[t], stats.at[t], stat_sem.at[0], stat_sem.at[1], peer, MESH
        ).start()
    pack(0)
    wait_bytes(stats.at[pl.ds(0, 15)], stat_sem.at[1])
    total = stats[0]
    for i in range(1, 16):
        total = total + stats[i]
    scale = lax.rsqrt(total[:1] * (1.0 / 8192.0) + epsilon)
    wide = jnp.transpose(tokens[...].astype(F32))
    own[...] = (wide * scale).astype(BF16)
    mine = gathered.at[x, a, c, b]
    for d in (1, 3, 2):
        pltpu.make_async_remote_copy(
            own, mine, a_sem.at[0], a_sem.at[1], at_ab((a + d) % 4, b), MESH
        ).start()
    local = pltpu.make_async_copy(own, mine, local_sem)
    local.start()
    pack(1)
    local.wait()
    wait_bytes(gathered.at[x, pl.ds(0, 3), c, b], a_sem.at[1])
    column = gathered.at[x, :, c, b]
    for i, d in enumerate((1, 3, 2)):
        pltpu.make_async_remote_copy(
            column, column, b_send, b_recv.at[i], at_ab(a, (b + d) % 4), MESH
        ).start()
    send_column(0)
    send_wave(0)
    send_column(1)
    send_column(2)
    send_column(3)
    send_wave(1)
    pack(2)
    pass_on(0)
    send_wave(2)
    pack(3)
    pass_on(1)
    take_across(0)
    send_wave(3)
    pass_on(2)
    take_across(1)
    pass_on(3)
    take_across(2)
    take_across(3)
    wait_bytes(gathered.at[:, :, 1 - c], d_recv)
    loads = [
        pltpu.make_async_copy(gathered.at[:, x, 0], slab_t.at[0], local_sem),
        pltpu.make_async_copy(gathered.at[:, :, 1, x], slab_t.at[1], a_sem.at[1]),
    ]
    for load in loads:
        load.start()
    for load in loads:
        load.wait()

    @pl.loop(0, 4)
    def _(from_x):
        for from_c in range(2):
            for from_z in range(4):
                dp = from_x * 2 + from_z % 2
                rows = pl.ds(pl.multiple_of(dp * 128, 128), 128)
                slab[(from_z // 2) * 2 + from_c, rows, :] = jnp.transpose(slab_t[from_c, from_x, from_z])

    wait_bytes(arrived.at[0], wave_recv.at[0])
    for half in range(2):
        sent[0, half] = forward(0, half).astype(BF16)
        pass_copy(half).start()
    wait_bytes(arrived.at[1], wave_recv.at[1])
    sent[1, 1] = forward(1, 1).astype(BF16)
    partial_copy(1, 1).start()
    wait_bytes(arrived.at[2], wave_recv.at[2])
    sent[2, 0] = forward(2, 0).astype(BF16)
    partial_copy(2, 0).start()
    held[0] = forward(1, 0)
    held[1] = forward(2, 1)
    pass_copy(0).wait_recv()
    sent[1, 0] = (held[0] + passing[0].astype(F32)).astype(BF16)
    partial_copy(1, 0).start()
    pass_copy(1).wait_recv()
    sent[2, 1] = (held[1] + passing[1].astype(F32)).astype(BF16)
    partial_copy(2, 1).start()
    wait_bytes(arrived.at[3], wave_recv.at[3])
    for half in range(2):
        sums[half] = forward(3, half)

    for w, half in ((1, 1), (2, 0), (1, 0), (2, 1)):
        partial_copy(w, half).wait_recv()

    for half in range(2):
        @pl.loop(0, 2)
        def _(part):
            rows = pl.ds(pl.multiple_of(part * 256, 256), 256)
            total = sums[half, rows, :] + (got[0, half, rows, :].astype(F32) + got[1, half, rows, :].astype(F32))
            to = pl.ds(pl.multiple_of(half * 512 + part * 256, 256), 256)
            gate_term, up_term = hidden_terms(total, adjoint[to, :])
            terms[to, :128] = gate_term
            terms[to, 128:] = up_term

    for half in range(2):
        pass_copy(half).wait_send()
        for w in (1, 2):
            partial_copy(w, half).wait_send()
    for w in range(4):
        wait_bytes(packed.at[w, pl.ds(0, 15)], wave_send.at[w])
    for w in (2, 3):
        their_copy(w).wait_send()
    wait_bytes(stats.at[pl.ds(0, 15)], stat_sem.at[0])
    wait_bytes(gathered.at[0, 0, 0, pl.ds(0, 3)], a_sem.at[0])
    wait_bytes(gathered.at[0, pl.ds(0, 3), 0], b_send)
    wait_bytes(gathered.at[0], x_send)
    wait_bytes(gathered.at[0, pl.ds(0, 2)], f_send)
    wait_bytes(gathered.at[pl.ds(0, 2)], d_send)


def product(gathered, terms, gate, up, blocks, gate_out, up_out, in_sem, out_sem):
    def load(t):
        row, pair = t // 4, ((t // 2) % 2) * 2
        if t % 2 == 0:
            return pltpu.make_async_copy(
                gathered.at[:, row, 0, pl.ds(pair, 2)], blocks.at[t], in_sem.at[t]
            )
        return pltpu.make_async_copy(
            gathered.at[:, pl.ds(pair, 2), 1, row], blocks.at[t], in_sem.at[t]
        )

    def stores(t):
        rows = pl.ds(512 * t, 512)
        return (
            pltpu.make_async_copy(gate_out.at[t], gate.at[rows], out_sem.at[0, t]),
            pltpu.make_async_copy(up_out.at[t], up.at[rows], out_sem.at[1, t]),
        )

    for t in range(16):
        load(t).start()
    for t in range(16):
        load(t).wait()
        lhs = jnp.concatenate([blocks[t, i, j] for i in range(4) for j in range(2)], axis=1)
        result = jnp.dot(lhs, terms[...], preferred_element_type=F32)
        gate_out[t] = result[:, :128]
        up_out[t] = result[:, 128:]
        for store in stores(t):
            store.start()
    for t in range(16):
        for store in stores(t):
            store.wait()


def local(tokens, gate_weight, up_weight, gate_tangent, up_tangent, adjoint):
    dma = pltpu.SemaphoreType.DMA
    gathered, terms = pl.pallas_call(
        exchange,
        out_shape=(
            jax.ShapeDtypeStruct((4, 4, 2, 4, 512, 128), BF16),
            jax.ShapeDtypeStruct((1024, 256), BF16),
        ),
        in_specs=[pl.BlockSpec(memory_space=pltpu.VMEM)] * 2 + [pl.BlockSpec(memory_space=pl.ANY)] * 4,
        out_specs=(pl.BlockSpec(memory_space=pl.ANY), pl.BlockSpec(memory_space=pltpu.VMEM)),
        scratch_shapes=[
            pltpu.VMEM((2, 4, 64, 4096), BF16),
            pltpu.VMEM((2, 16, 4, 64, 128), BF16),
            pltpu.VMEM((4, 16, 4, 128, 128), BF16),
            pltpu.VMEM((4, 16, 4, 128, 128), BF16),
            pltpu.VMEM((16, 8, 128), F32),
            pltpu.VMEM((512, 128), BF16),
            pltpu.VMEM((2, 4, 4, 512, 128), BF16),
            pltpu.VMEM((4, 1024, 512), BF16),
            pltpu.VMEM((2, 512, 512), F32),
            pltpu.VMEM((2, 512, 512), F32),
            pltpu.VMEM((3, 2, 512, 512), BF16),
            pltpu.VMEM((2, 512, 512), BF16),
            pltpu.VMEM((2, 2, 512, 512), BF16),
            dma((2, 4)), dma((2,)), dma((4,)), dma((4,)), dma((4,)), dma((2,)), dma,
            dma((2,)), dma, dma((3,)), dma, dma((4,)), dma((4,)), dma, dma((4,)), dma((4,)), dma, dma,
            dma((2,)), dma((2,)), dma((2, 2)), dma((2, 2)),
        ],
        compiler_params=pltpu.CompilerParams(
            collective_id=0, has_side_effects=True, vmem_limit_bytes=58 * 2**20
        ),
        name="exchange",
    )(tokens, adjoint, gate_weight, up_weight, gate_tangent, up_tangent)

    return pl.pallas_call(
        product,
        out_shape=(jax.ShapeDtypeStruct((8192, 128), F32),) * 2,
        in_specs=[pl.BlockSpec(memory_space=pl.ANY), pl.BlockSpec(memory_space=pltpu.VMEM)],
        out_specs=(pl.BlockSpec(memory_space=pl.ANY),) * 2,
        scratch_shapes=[
            pltpu.VMEM((16, 4, 2, 512, 128), BF16),
            pltpu.VMEM((16, 512, 128), F32),
            pltpu.VMEM((16, 512, 128), F32),
            dma((16,)), dma((2, 16)),
        ],
        compiler_params=pltpu.CompilerParams(vmem_limit_bytes=58 * 2**20),
        name="product",
    )(gathered, terms)


def solution(mesh):
    in_specs = (
        P("dp", "tensor"),
        P(("dp", "tensor"), None),
        P(("dp", "tensor"), None),
        P(("dp", "tensor"), None),
        P(("dp", "tensor"), None),
        P(None, ("dp", "tensor")),
    )
    out_specs = (P(None, ("dp", "tensor")), P(None, ("dp", "tensor")))
    return jax.shard_map(local, mesh=mesh, in_specs=in_specs, out_specs=out_specs, check_vma=False)
```

time: 218 us -> 155 us (0.71)
  Pallas kernels: 216 us -> 153 us
    pallas_call x1, Pallas kernels: 200 us -> 139 us  [local(): pl.pallas_call(exchange, out_shape=(jax.ShapeDtypeStruct((4, 4, 2, 4, 512...]
    pallas_call x1, Pallas kernels: 16.8 us -> 14.5 us  [local(): pl.pallas_call(product, out_shape=(jax.ShapeDtypeStruct((8192, 128), F32)...]
where the time goes in v2:
time: 155 us; the launch traced here: 154 us
  Pallas kernels  153 us (99%)
    pallas_call x1, Pallas kernels, local(): pl.pallas_call(exchange, out_shape=(jax.ShapeDtypeStruct((4, 4, 2, 4, 512...  139 us
    pallas_call x1, Pallas kernels, local(): pl.pallas_call(product, out_shape=(jax.ShapeDtypeStruct((8192, 128), F32)...  14.5 us

profile of v2, /device:TPU:1, one launch (start us, length us, event | category | flops | bytes accessed | tf_op | source)
XLA Modules:
  0.0 153.9 jit_solution(1944704281587674575)
XLA Ops:
  0.6 138.6 %exchange.1 = (bf16[4,4,2,4,512,128]{5,4,3,2,1,0:T(8,128)(2,1)}, bf16[1024,256]{1,0:T(8,128)(2,1)}) custom-call(bf16[128,512]{1,0:T(8,128)(2,1)} %tokens.1, bf16[1024,128]{1,0:T(8,128)(2,1)} %adjoint.1, bf16[64,16384]{1,0:T(8,128)(2,1)} %w0.1, bf16[64,16384]{1,0:T(8,128)(2,1)} %w1.1, bf16[64,16384]{1,0:T(8,128)(2,1)} %w2.1, bf16[64,16384]{1,0:T(8,128)(2,1)} %w3.1), custom_call_target="tpu_custom_call" | custom-call | tf_op jit(solution)/shard_map/exchange/pallas_call | solution.py:334
  139.2 14.5 %product.1 = (f32[8192,128]{1,0:T(8,128)}, f32[8192,128]{1,0:T(8,128)}) custom-call(bf16[4,4,2,4,512,128]{5,4,3,2,1,0:T(8,128)(2,1)} %get-tuple-element.4.gathered, bf16[1024,256]{1,0:T(8,128)(2,1)} %get-tuple-element.5.terms), custom_call_target="tpu_custom_call" | custom-call | tf_op jit(solution)/shard_map/product/pallas_call | solution.py:366

commit v3 on v2

--- a/solution.py
+++ b/solution.py
@@ -296,17 +296,7 @@
     wait_bytes(gathered.at[pl.ds(0, 2)], d_send)
 
 
-def product(gathered, terms, gate, up, blocks, gate_out, up_out, in_sem, out_sem):
-    def load(t):
-        row, pair = t // 4, ((t // 2) % 2) * 2
-        if t % 2 == 0:
-            return pltpu.make_async_copy(
-                gathered.at[:, row, 0, pl.ds(pair, 2)], blocks.at[t], in_sem.at[t]
-            )
-        return pltpu.make_async_copy(
-            gathered.at[:, pl.ds(pair, 2), 1, row], blocks.at[t], in_sem.at[t]
-        )
-
+def product(gathered, terms, gate, up, gate_out, up_out, out_sem):
     def stores(t):
         rows = pl.ds(512 * t, 512)
         return (
@@ -315,10 +305,15 @@
         )
 
     for t in range(16):
-        load(t).start()
-    for t in range(16):
-        load(t).wait()
-        lhs = jnp.concatenate([blocks[t, i, j] for i in range(4) for j in range(2)], axis=1)
+        row, pair = t // 4, ((t // 2) % 2) * 2
+        lhs = jnp.concatenate(
+            [
+                gathered[i, row, 0, pair + j] if t % 2 == 0 else gathered[i, pair + j, 1, row]
+                for i in range(4)
+                for j in range(2)
+            ],
+            axis=1,
+        )
         result = jnp.dot(lhs, terms[...], preferred_element_type=F32)
         gate_out[t] = result[:, :128]
         up_out[t] = result[:, 128:]
@@ -334,8 +329,8 @@
     gathered, terms = pl.pallas_call(
         exchange,
         out_shape=(
-            jax.ShapeDtypeStruct((4, 4, 2, 4, 512, 128), BF16),
-            jax.ShapeDtypeStruct((1024, 256), BF16),
+            pltpu.VMEM((4, 4, 2, 4, 512, 128), BF16),
+            pltpu.VMEM((1024, 256), BF16),
         ),
         in_specs=[pl.BlockSpec(memory_space=pltpu.VMEM)] * 2 + [pl.BlockSpec(memory_space=pl.ANY)] * 4,
         out_specs=(pl.BlockSpec(memory_space=pl.ANY), pl.BlockSpec(memory_space=pltpu.VMEM)),
@@ -358,23 +353,24 @@
             dma((2,)), dma((2,)), dma((2, 2)), dma((2, 2)),
         ],
         compiler_params=pltpu.CompilerParams(
-            collective_id=0, has_side_effects=True, vmem_limit_bytes=58 * 2**20
+            collective_id=0, has_side_effects=True, vmem_limit_bytes=44 * 2**20
         ),
         name="exchange",
     )(tokens, adjoint, gate_weight, up_weight, gate_tangent, up_tangent)
 
+    gathered = pltpu.with_memory_space_constraint(gathered, pltpu.VMEM)
+    terms = pltpu.with_memory_space_constraint(terms, pltpu.VMEM)
     return pl.pallas_call(
         product,
         out_shape=(jax.ShapeDtypeStruct((8192, 128), F32),) * 2,
-        in_specs=[pl.BlockSpec(memory_space=pl.ANY), pl.BlockSpec(memory_space=pltpu.VMEM)],
+        in_specs=[pl.BlockSpec(memory_space=pltpu.VMEM)] * 2,
         out_specs=(pl.BlockSpec(memory_space=pl.ANY),) * 2,
         scratch_shapes=[
-            pltpu.VMEM((16, 4, 2, 512, 128), BF16),
             pltpu.VMEM((16, 512, 128), F32),
             pltpu.VMEM((16, 512, 128), F32),
-            dma((16,)), dma((2, 16)),
+            dma((2, 16)),
         ],
-        compiler_params=pltpu.CompilerParams(vmem_limit_bytes=58 * 2**20),
+        compiler_params=pltpu.CompilerParams(vmem_limit_bytes=24 * 2**20),
         name="product",
     )(gathered, terms)
 

time: 155 us -> 147 us (0.948)
  Pallas kernels: 153 us -> 144 us
    pallas_call x1, Pallas kernels: 14.5 us -> 6.03 us  [local(): pl.pallas_call(product, out_shape=(jax.ShapeDtypeStruct((8192, 128), F32)...]
where the time goes in v3:
time: 147 us; the launch traced here: 145 us
  Pallas kernels  144 us (98%)
    pallas_call x1, Pallas kernels, local(): pl.pallas_call(exchange, out_shape=(pltpu.VMEM((4, 4, 2, 4, 512, 128), BF...  138 us
    pallas_call x1, Pallas kernels, local(): pl.pallas_call(product, out_shape=(jax.ShapeDtypeStruct((8192, 128), F32)...  6.03 us

profile of v3, /device:TPU:1, one launch (start us, length us, event | category | flops | bytes accessed | tf_op | source)
XLA Modules:
  0.0 144.6 jit_solution(15426506006167281803)
XLA Ops:
  0.6 138.0 %exchange.1 = (bf16[4,4,2,4,512,128]{5,4,3,2,1,0:T(8,128)(2,1)S(1)}, bf16[1024,256]{1,0:T(8,128)(2,1)S(1)}) custom-call(bf16[128,512]{1,0:T(8,128)(2,1)} %tokens.1, bf16[1024,128]{1,0:T(8,128)(2,1)} %adjoint.1, bf16[64,16384]{1,0:T(8,128)(2,1)} %w0.1, bf16[64,16384]{1,0:T(8,128)(2,1)} %w1.1, bf16[64,16384]{1,0:T(8,128)(2,1)} %w2.1, bf16[64,16384]{1,0:T(8,128)(2,1)} %w3.1), custom_call_target="tpu_custom_call" | custom-call | tf_op jit(solution)/shard_map/exchange/pallas_call | solution.py:329
  138.6 6.0 %product.1 = (f32[8192,128]{1,0:T(8,128)}, f32[8192,128]{1,0:T(8,128)}) custom-call(bf16[4,4,2,4,512,128]{5,4,3,2,1,0:T(8,128)(2,1)S(1)} %get-tuple-element.4.gathered, bf16[1024,256]{1,0:T(8,128)(2,1)S(1)} %get-tuple-element.5.terms), custom_call_target="tpu_custom_call" | custom-call | tf_op jit(solution)/shard_map/product/pallas_call | solution.py:363

commit v4 on v3

--- a/solution.py
+++ b/solution.py
@@ -42,9 +42,9 @@
 
 def exchange(
     tokens, adjoint, w0, w1, w2, w3, gathered, terms,
-    staged, theirs, packed, arrived, stats, own, slab_t, slab, sums, held, sent, passing, got,
-    stage_sem, their_send, their_recv, wave_send, wave_recv, stat_sem, local_sem,
-    a_sem, b_send, b_recv, x_send, x_left, x_right, f_send, f_left, f_right, d_send, d_recv,
+    staged, theirs, packed, arrived, stats, scales, slab, sums, held, sent, passing, got,
+    stage_sem, their_send, their_recv, wave_send, wave_recv, stat_sem, scale_sem,
+    a_send, a_recv, b_send, b_recv, x_send, x_left, x_right, f_send, f_left, f_right, d_send, d_recv,
     pass_send, pass_recv, p_send, p_recv,
 ):
     weights = (w0, w1, w2, w3)
@@ -95,14 +95,14 @@
                 packed[w, q, m, pl.ds(pl.multiple_of(c * 64, 64), 64), :] = jnp.where(c == 0, low, high)
                 theirs[w % 2, q, m] = jnp.where(c == 0, high, low)
 
-        their_copy(w).start()
         if w + 2 < 4:
             stage(w + 2)
 
     def send_wave(w):
         their_copy(w).wait_recv()
         for dy, dz in PLANE:
-            to_y, to_z = (y + dy) % 4, (z + dz) % 4
+            to_y = (y + dy * (1 - c) + (4 - dz) * c) % 4
+            to_z = (z + dz * (1 - c) + (4 - dy) * c) % 4
             pltpu.make_async_remote_copy(
                 packed.at[w, chip_in_plane(to_y, to_z)],
                 arrived.at[w, me],
@@ -121,13 +121,33 @@
 
     column_b = [b, (b + 3) % 4, (b + 1) % 4, (b + 2) % 4]
 
+    def send_x(i, block):
+        pltpu.make_async_remote_copy(block, block, x_send, x_left.at[i], to_right, MESH).start()
+        pltpu.make_async_remote_copy(block, block, x_send, x_right.at[i], to_left, MESH).start()
+
+    def send_block(at_a):
+        block = gathered.at[x, at_a, c, b]
+        for i, d in enumerate((1, 3, 2)):
+            pltpu.make_async_remote_copy(
+                block, block, b_send, b_recv.at[i], at_ab(a, (b + d) % 4), MESH
+            ).start()
+        send_x(0, block)
+
     def send_column(i):
         block = gathered.at[x, :, c, column_b[i]]
-        if i > 0:
-            wait_bytes(block, b_recv.at[i - 1])
-        pltpu.make_async_remote_copy(block, block, x_send, x_left.at[i], to_right, MESH).start()
-        pltpu.make_async_remote_copy(block, block, x_send, x_right.at[i], to_left, MESH).start()
+        wait_bytes(block, b_recv.at[i - 1])
+        send_x(i, block)
         share(block)
+
+    def normalise(from_x):
+        @pl.loop(0, 16)
+        def _(i):
+            at_a, at_b = i // 4, i % 4
+            for from_c in range(2):
+                from_z = at_a if from_c else at_b
+                scale = scales[from_x * 2 + from_z % 2][:1]
+                block = gathered[from_x, at_a, from_c, at_b].astype(F32)
+                gathered[from_x, at_a, from_c, at_b] = (block * scale).astype(BF16)
 
     def pass_on(i):
         block = gathered.at[left, :, c, column_b[i]]
@@ -174,51 +194,58 @@
     cross_peers = [
         device(x, (y + dy) % 4, (z + dz) % 4, 1 - c) for dy in range(4) for dz in (0, 2)
     ]
-    everyone = peers + cross_peers + [to_right, to_left]
+    flipped = z + 1 - 2 * (z % 2)
+    dp_peers = [device((x + dx) % 4, y, flipped, c) for dx in (1, 2, 3)]
+    x_peers = [device((x + dx) % 4, y, z, c) for dx in (1, 2, 3)]
+    everyone = peers + cross_peers + x_peers + dp_peers
     for peer in everyone:
         pl.semaphore_signal(barrier, 1, device_id=peer, device_id_type=MESH)
 
-    wide = jnp.transpose(tokens[...].astype(F32))
+    turned = jnp.transpose(tokens[...])
+    gathered[x, a, c, b] = turned
+    wide = turned.astype(F32)
     t = lax.axis_index("tensor")
     stats[t] = jnp.broadcast_to(jnp.sum(wide * wide, axis=0, keepdims=True), (8, 128))
+    pack(0)
     pl.semaphore_wait(barrier, len(everyone))
+    mine = gathered.at[x, a, c, b]
+    for i, d in enumerate((1, 3, 2)):
+        pltpu.make_async_remote_copy(
+            mine, mine, a_send, a_recv.at[i], at_ab((a + d) % 4, b), MESH
+        ).start()
+    send_block(a)
+    their_copy(0).start()
     for peer in stat_peers:
         pltpu.make_async_remote_copy(
             stats.at[t], stats.at[t], stat_sem.at[0], stat_sem.at[1], peer, MESH
         ).start()
-    pack(0)
+    pack(1)
+    their_copy(1).start()
+    for i, d in enumerate((3, 1, 2)):
+        wait_bytes(gathered.at[x, (a + d) % 4, c, b], a_recv.at[i])
+        send_block((a + d) % 4)
+    share(gathered.at[x, :, c, b])
+    send_wave(0)
     wait_bytes(stats.at[pl.ds(0, 15)], stat_sem.at[1])
     total = stats[0]
     for i in range(1, 16):
         total = total + stats[i]
-    scale = lax.rsqrt(total[:1] * (1.0 / 8192.0) + epsilon)
-    wide = jnp.transpose(tokens[...].astype(F32))
-    own[...] = (wide * scale).astype(BF16)
-    mine = gathered.at[x, a, c, b]
-    for d in (1, 3, 2):
+    dp = lax.axis_index("dp")
+    scales[dp] = lax.rsqrt(total * (1.0 / 8192.0) + epsilon)
+    for peer in x_peers + dp_peers + [device(x, y, flipped, c)]:
         pltpu.make_async_remote_copy(
-            own, mine, a_sem.at[0], a_sem.at[1], at_ab((a + d) % 4, b), MESH
+            scales.at[dp], scales.at[dp], scale_sem.at[0], scale_sem.at[1], peer, MESH
         ).start()
-    local = pltpu.make_async_copy(own, mine, local_sem)
-    local.start()
-    pack(1)
-    local.wait()
-    wait_bytes(gathered.at[x, pl.ds(0, 3), c, b], a_sem.at[1])
-    column = gathered.at[x, :, c, b]
-    for i, d in enumerate((1, 3, 2)):
-        pltpu.make_async_remote_copy(
-            column, column, b_send, b_recv.at[i], at_ab(a, (b + d) % 4), MESH
-        ).start()
-    send_column(0)
-    send_wave(0)
     send_column(1)
     send_column(2)
     send_column(3)
     send_wave(1)
     pack(2)
+    their_copy(2).start()
     pass_on(0)
     send_wave(2)
     pack(3)
+    their_copy(3).start()
     pass_on(1)
     take_across(0)
     send_wave(3)
@@ -228,14 +255,7 @@
     take_across(2)
     take_across(3)
     wait_bytes(gathered.at[:, :, 1 - c], d_recv)
-    loads = [
-        pltpu.make_async_copy(gathered.at[:, x, 0], slab_t.at[0], local_sem),
-        pltpu.make_async_copy(gathered.at[:, :, 1, x], slab_t.at[1], a_sem.at[1]),
-    ]
-    for load in loads:
-        load.start()
-    for load in loads:
-        load.wait()
+    wait_bytes(scales.at[pl.ds(0, 7)], scale_sem.at[1])
 
     @pl.loop(0, 4)
     def _(from_x):
@@ -243,7 +263,9 @@
             for from_z in range(4):
                 dp = from_x * 2 + from_z % 2
                 rows = pl.ds(pl.multiple_of(dp * 128, 128), 128)
-                slab[(from_z // 2) * 2 + from_c, rows, :] = jnp.transpose(slab_t[from_c, from_x, from_z])
+                block = gathered[from_x, from_z, 1, x] if from_c else gathered[from_x, x, 0, from_z]
+                block = (block.astype(F32) * scales[dp][:1]).astype(BF16)
+                slab[(from_z // 2) * 2 + from_c, rows, :] = jnp.transpose(block)
 
     wait_bytes(arrived.at[0], wave_recv.at[0])
     for half in range(2):
@@ -257,12 +279,21 @@
     partial_copy(2, 0).start()
     held[0] = forward(1, 0)
     held[1] = forward(2, 1)
+    wait_bytes(gathered.at[0, 0, 0, pl.ds(0, 3)], a_send)
+    wait_bytes(gathered.at[0, pl.ds(0, 3), 0], b_send)
+    wait_bytes(gathered.at[0], x_send)
+    wait_bytes(gathered.at[0, pl.ds(0, 2)], f_send)
+    wait_bytes(gathered.at[pl.ds(0, 2)], d_send)
+    normalise(0)
+    normalise(1)
     pass_copy(0).wait_recv()
     sent[1, 0] = (held[0] + passing[0].astype(F32)).astype(BF16)
     partial_copy(1, 0).start()
     pass_copy(1).wait_recv()
     sent[2, 1] = (held[1] + passing[1].astype(F32)).astype(BF16)
     partial_copy(2, 1).start()
+    normalise(2)
+    normalise(3)
     wait_bytes(arrived.at[3], wave_recv.at[3])
     for half in range(2):
         sums[half] = forward(3, half)
@@ -289,11 +320,7 @@
     for w in (2, 3):
         their_copy(w).wait_send()
     wait_bytes(stats.at[pl.ds(0, 15)], stat_sem.at[0])
-    wait_bytes(gathered.at[0, 0, 0, pl.ds(0, 3)], a_sem.at[0])
-    wait_bytes(gathered.at[0, pl.ds(0, 3), 0], b_send)
-    wait_bytes(gathered.at[0], x_send)
-    wait_bytes(gathered.at[0, pl.ds(0, 2)], f_send)
-    wait_bytes(gathered.at[pl.ds(0, 2)], d_send)
+    wait_bytes(scales.at[pl.ds(0, 7)], scale_sem.at[0])
 
 
 def product(gathered, terms, gate, up, gate_out, up_out, out_sem):
@@ -333,23 +360,22 @@
             pltpu.VMEM((1024, 256), BF16),
         ),
         in_specs=[pl.BlockSpec(memory_space=pltpu.VMEM)] * 2 + [pl.BlockSpec(memory_space=pl.ANY)] * 4,
-        out_specs=(pl.BlockSpec(memory_space=pl.ANY), pl.BlockSpec(memory_space=pltpu.VMEM)),
+        out_specs=(pl.BlockSpec(memory_space=pltpu.VMEM),) * 2,
         scratch_shapes=[
             pltpu.VMEM((2, 4, 64, 4096), BF16),
             pltpu.VMEM((2, 16, 4, 64, 128), BF16),
             pltpu.VMEM((4, 16, 4, 128, 128), BF16),
             pltpu.VMEM((4, 16, 4, 128, 128), BF16),
             pltpu.VMEM((16, 8, 128), F32),
-            pltpu.VMEM((512, 128), BF16),
-            pltpu.VMEM((2, 4, 4, 512, 128), BF16),
+            pltpu.VMEM((8, 8, 128), F32),
             pltpu.VMEM((4, 1024, 512), BF16),
             pltpu.VMEM((2, 512, 512), F32),
             pltpu.VMEM((2, 512, 512), F32),
             pltpu.VMEM((3, 2, 512, 512), BF16),
             pltpu.VMEM((2, 512, 512), BF16),
             pltpu.VMEM((2, 2, 512, 512), BF16),
-            dma((2, 4)), dma((2,)), dma((4,)), dma((4,)), dma((4,)), dma((2,)), dma,
-            dma((2,)), dma, dma((3,)), dma, dma((4,)), dma((4,)), dma, dma((4,)), dma((4,)), dma, dma,
+            dma((2, 4)), dma((2,)), dma((4,)), dma((4,)), dma((4,)), dma((2,)), dma((2,)),
+            dma, dma((3,)), dma, dma((3,)), dma, dma((4,)), dma((4,)), dma, dma((4,)), dma((4,)), dma, dma,
             dma((2,)), dma((2,)), dma((2, 2)), dma((2, 2)),
         ],
         compiler_params=pltpu.CompilerParams(

time: 147 us -> 135 us (0.918); the launches traced: 145 us -> 134 us
  Pallas kernels: 144 us -> 134 us
    pallas_call x1, Pallas kernels: 138 us -> 128 us  [local(): pl.pallas_call(exchange, out_shape=(pltpu.VMEM((4, 4, 2, 4, 512, 128), BF...]
where the time goes in v4:
time: 135 us; the launch traced here: 134 us
  Pallas kernels  134 us (99%)
    pallas_call x1, Pallas kernels, local(): pl.pallas_call(exchange, out_shape=(pltpu.VMEM((4, 4, 2, 4, 512, 128), BF...  128 us
    pallas_call x1, Pallas kernels, local(): pl.pallas_call(product, out_shape=(jax.ShapeDtypeStruct((8192, 128), F32)...  6.03 us

profile of v4, /device:TPU:1, one launch (start us, length us, event | category | flops | bytes accessed | tf_op | source)
XLA Modules:
  0.0 134.2 jit_solution(551958724153015640)
XLA Ops:
  0.6 127.5 %exchange.1 = (bf16[4,4,2,4,512,128]{5,4,3,2,1,0:T(8,128)(2,1)S(1)}, bf16[1024,256]{1,0:T(8,128)(2,1)S(1)}) custom-call(bf16[128,512]{1,0:T(8,128)(2,1)} %tokens.1, bf16[1024,128]{1,0:T(8,128)(2,1)} %adjoint.1, bf16[64,16384]{1,0:T(8,128)(2,1)} %w0.1, bf16[64,16384]{1,0:T(8,128)(2,1)} %w1.1, bf16[64,16384]{1,0:T(8,128)(2,1)} %w2.1, bf16[64,16384]{1,0:T(8,128)(2,1)} %w3.1), custom_call_target="tpu_custom_call" | custom-call | tf_op jit(solution)/shard_map/exchange/pallas_call | solution.py:356
  128.2 6.0 %product.1 = (f32[8192,128]{1,0:T(8,128)}, f32[8192,128]{1,0:T(8,128)}) custom-call(bf16[4,4,2,4,512,128]{5,4,3,2,1,0:T(8,128)(2,1)S(1)} %get-tuple-element.4.gathered, bf16[1024,256]{1,0:T(8,128)(2,1)S(1)} %get-tuple-element.5.terms), custom_call_target="tpu_custom_call" | custom-call | tf_op jit(solution)/shard_map/product/pallas_call | solution.py:389

commit v5 on v4

--- a/solution.py
+++ b/solution.py
@@ -12,7 +12,12 @@
     (1, 0), (0, 1), (3, 0), (0, 3), (2, 0), (0, 2), (1, 1), (3, 3),
     (1, 3), (3, 1), (1, 2), (2, 1), (3, 2), (2, 3), (2, 2),
 )
-WAVES = (2, 1, 3, 0)
+WAVES = (
+    ((0, 2), (1, 2), (2, 2), (3, 2)),
+    ((0, 1), (1, 1), (0, 3), (1, 3)),
+    ((2, 1), (3, 1), (2, 3), (3, 3)),
+    ((0, 0), (1, 0), (2, 0), (3, 0)),
+)
 
 
 def place():
@@ -42,8 +47,8 @@
 
 def exchange(
     tokens, adjoint, w0, w1, w2, w3, gathered, terms,
-    staged, theirs, packed, arrived, stats, scales, slab, sums, held, sent, passing, got,
-    stage_sem, their_send, their_recv, wave_send, wave_recv, stat_sem, scale_sem,
+    held_tokens, held_adjoint, staged, theirs, packed, arrived, stats, scales, slab, sums, held, sent, passing, part, got,
+    load_sem, stage_sem, their_send, their_recv, wave_send, wave_recv, stat_sem, scale_sem,
     a_send, a_recv, b_send, b_recv, x_send, x_left, x_right, f_send, f_left, f_right, d_send, d_recv,
     pass_send, pass_recv, p_send, p_recv,
 ):
@@ -59,13 +64,17 @@
         return device(x, to_a * (1 - c) + to_b * c, to_b * (1 - c) + to_a * c, c)
 
     def stage_copies(w):
-        start = pl.multiple_of(((x + WAVES[w]) % 4) * 4096, 4096)
-        return [
-            pltpu.make_async_copy(
-                weights[m].at[:, pl.ds(start, 4096)], staged.at[w % 2, m], stage_sem.at[w % 2, m]
+        copies = []
+        for slot, (m, owner) in enumerate(WAVES[w]):
+            start = pl.multiple_of(((x + owner) % 4) * 4096, 4096)
+            copies.append(
+                pltpu.make_async_copy(
+                    weights[m].at[:, pl.ds(start, 4096)],
+                    staged.at[w % 2, slot],
+                    stage_sem.at[w % 2, slot],
+                )
             )
-            for m in range(4)
-        ]
+        return copies
 
     def stage(w):
         for copy in stage_copies(w):
@@ -116,8 +125,8 @@
     def wait_bytes(ref, sem):
         pltpu.make_async_copy(ref, ref, sem).wait()
 
-    def share(block):
-        pltpu.make_async_remote_copy(block, block, d_send, d_recv, partner, MESH).start()
+    def share(block, r):
+        pltpu.make_async_remote_copy(block, block, d_send, d_recv.at[r], partner, MESH).start()
 
     column_b = [b, (b + 3) % 4, (b + 1) % 4, (b + 2) % 4]
 
@@ -125,19 +134,22 @@
         pltpu.make_async_remote_copy(block, block, x_send, x_left.at[i], to_right, MESH).start()
         pltpu.make_async_remote_copy(block, block, x_send, x_right.at[i], to_left, MESH).start()
 
-    def send_block(at_a):
-        block = gathered.at[x, at_a, c, b]
+    block_a = [a, (a + 3) % 4, (a + 1) % 4, (a + 2) % 4]
+
+    def send_block(k):
+        block = gathered.at[x, block_a[k], c, b]
+        if k > 0:
+            wait_bytes(block, a_recv.at[k - 1])
         for i, d in enumerate((1, 3, 2)):
             pltpu.make_async_remote_copy(
-                block, block, b_send, b_recv.at[i], at_ab(a, (b + d) % 4), MESH
+                block, block, b_send, b_recv.at[i, k], at_ab(a, (b + d) % 4), MESH
             ).start()
         send_x(0, block)
 
-    def send_column(i):
-        block = gathered.at[x, :, c, column_b[i]]
-        wait_bytes(block, b_recv.at[i - 1])
+    def relay_block(i, k):
+        block = gathered.at[x, block_a[k], c, column_b[i]]
+        wait_bytes(block, b_recv.at[i - 1, k])
         send_x(i, block)
-        share(block)
 
     def normalise(from_x):
         @pl.loop(0, 16)
@@ -154,37 +166,66 @@
         wait_bytes(block, x_left.at[i])
         half = gathered.at[left, pl.ds(0, 2), c, column_b[i]]
         pltpu.make_async_remote_copy(half, half, f_send, f_left.at[i], to_right, MESH).start()
-        share(block)
+        share(block, 1)
         block = gathered.at[right, :, c, column_b[i]]
         wait_bytes(block, x_right.at[i])
         half = gathered.at[right, pl.ds(2, 2), c, column_b[i]]
         pltpu.make_async_remote_copy(half, half, f_send, f_right.at[i], to_left, MESH).start()
-        share(block)
+        share(block, 2)
 
     def take_across(i):
         wait_bytes(gathered.at[across, pl.ds(0, 2), c, column_b[i]], f_left.at[i])
         wait_bytes(gathered.at[across, pl.ds(2, 2), c, column_b[i]], f_right.at[i])
-        share(gathered.at[across, :, c, column_b[i]])
-
-    def forward(w, half):
-        lhs = jnp.concatenate([slab[k, half * 512 : half * 512 + 512, :] for k in range(4)], axis=1)
+        share(gathered.at[across, :, c, column_b[i]], 3)
+
+    def forward(w, rows):
+        lhs = jnp.concatenate([slab[k, rows, :] for k in range(4)], axis=1)
         rhs = jnp.concatenate([arrived[w, :, m].reshape(2048, 128) for m in range(4)], axis=1)
         return jnp.dot(lhs, rhs, preferred_element_type=F32)
 
-    def pass_copy(half):
+    def quarter(q):
+        return pl.ds(pl.multiple_of(q * 256, 256), 256)
+
+    def x_neighbour(way):
+        return device((x + 1 + 2 * way) % 4, y, z, c)
+
+    def make_slab(q, r):
+        wait_bytes(gathered.at[q, :, 1 - c], d_recv.at[r])
+        for from_z in range(4):
+            for from_c in range(2):
+                rows = pl.ds(pl.multiple_of(q * 256 + from_z % 2 * 128, 128), 128)
+                scale = scales[q * 2 + from_z % 2][:1]
+                block = gathered[q, from_z, 1, x] if from_c else gathered[q, x, 0, from_z]
+                block = (block.astype(F32) * scale).astype(BF16)
+                slab[(from_z // 2) * 2 + from_c, rows, :] = jnp.transpose(block)
+
+    def pass_copy(q):
         return pltpu.make_async_remote_copy(
-            sent.at[0, half], passing.at[half], pass_send.at[half], pass_recv.at[half],
-            to_left if half else to_right, MESH,
+            sent.at[q], passing.at[q], pass_send.at[q], pass_recv.at[q], x_neighbour(q // 2), MESH
         )
 
-    def partial_copy(w, half):
-        return pltpu.make_async_remote_copy(
-            sent.at[w, half], got.at[w - 1, half], p_send.at[w - 1, half], p_recv.at[w - 1, half],
-            to_left if w == 2 else to_right, MESH,
-        )
-
-    stage(0)
-    stage(1)
+    def forward_across(q):
+        sent[q] = forward(0, quarter(q)).astype(BF16)
+        pass_copy(q).start()
+
+    def part_copy(w, q, late, way):
+        pltpu.make_async_remote_copy(
+            part.at[w - 1, late, q], got.at[w - 1, way, q], p_send, p_recv.at[q], x_neighbour(way), MESH
+        ).start()
+
+    def forward_beside(w, q):
+        total = forward(w, quarter(q))
+        to_r, to_l = total[:, :256], total[:, 256:]
+        way = q // 2
+        part[w - 1, 0, q] = jnp.where(way == 0, to_l, to_r).astype(BF16)
+        part_copy(w, q, 0, 1 - way)
+        held[w - 1, q] = jnp.where(way == 0, to_r, to_l)
+
+    def add_passing(w, q):
+        add = passing[q, :, (w - 1) * 256 : w * 256].astype(F32)
+        part[w - 1, 1, q] = (held[w - 1, q] + add).astype(BF16)
+        part_copy(w, q, 1, q // 2)
+
     barrier = pltpu.get_barrier_semaphore()
     peers = [device(x, (y + dy) % 4, (z + dz) % 4, c) for dy, dz in PLANE]
     stat_peers = [
@@ -201,31 +242,41 @@
     for peer in everyone:
         pl.semaphore_signal(barrier, 1, device_id=peer, device_id_type=MESH)
 
-    turned = jnp.transpose(tokens[...])
-    gathered[x, a, c, b] = turned
-    wide = turned.astype(F32)
-    t = lax.axis_index("tensor")
-    stats[t] = jnp.broadcast_to(jnp.sum(wide * wide, axis=0, keepdims=True), (8, 128))
-    pack(0)
+    load_tokens = pltpu.make_async_copy(tokens, held_tokens, load_sem.at[0])
+    load_tokens.start()
+    load_adjoint = pltpu.make_async_copy(adjoint, held_adjoint, load_sem.at[1])
+    load_adjoint.start()
+    stage(0)
+    stage(1)
+    load_tokens.wait()
+    turned = jnp.transpose(held_tokens[...])
+    mine = gathered.at[x, a, c, b]
+    mine[...] = turned
     pl.semaphore_wait(barrier, len(everyone))
-    mine = gathered.at[x, a, c, b]
     for i, d in enumerate((1, 3, 2)):
         pltpu.make_async_remote_copy(
             mine, mine, a_send, a_recv.at[i], at_ab((a + d) % 4, b), MESH
         ).start()
-    send_block(a)
-    their_copy(0).start()
+    send_block(0)
+    wide = turned.astype(F32)
+    t = lax.axis_index("tensor")
+    stats[t] = jnp.broadcast_to(jnp.sum(wide * wide, axis=0, keepdims=True), (8, 128))
     for peer in stat_peers:
         pltpu.make_async_remote_copy(
             stats.at[t], stats.at[t], stat_sem.at[0], stat_sem.at[1], peer, MESH
         ).start()
+    pack(0)
+    their_copy(0).start()
+    send_block(1)
+    send_block(2)
+    relay_block(1, 0)
+    relay_block(2, 0)
+    send_block(3)
+    relay_block(3, 0)
+    share(gathered.at[x, :, c, b], 0)
+    send_wave(0)
     pack(1)
     their_copy(1).start()
-    for i, d in enumerate((3, 1, 2)):
-        wait_bytes(gathered.at[x, (a + d) % 4, c, b], a_recv.at[i])
-        send_block((a + d) % 4)
-    share(gathered.at[x, :, c, b])
-    send_wave(0)
     wait_bytes(stats.at[pl.ds(0, 15)], stat_sem.at[1])
     total = stats[0]
     for i in range(1, 16):
@@ -236,9 +287,11 @@
         pltpu.make_async_remote_copy(
             scales.at[dp], scales.at[dp], scale_sem.at[0], scale_sem.at[1], peer, MESH
         ).start()
-    send_column(1)
-    send_column(2)
-    send_column(3)
+    for k in (1, 2, 3):
+        for i in (1, 2, 3):
+            relay_block(i, k)
+    for i in (1, 2, 3):
+        share(gathered.at[x, :, c, column_b[i]], 0)
     send_wave(1)
     pack(2)
     their_copy(2).start()
@@ -246,75 +299,68 @@
     send_wave(2)
     pack(3)
     their_copy(3).start()
+    wait_bytes(scales.at[pl.ds(0, 7)], scale_sem.at[1])
+    make_slab(x, 0)
     pass_on(1)
     take_across(0)
     send_wave(3)
+    wait_bytes(arrived.at[0], wave_recv.at[0])
+    forward_across(x)
     pass_on(2)
     take_across(1)
     pass_on(3)
+    make_slab(left, 1)
+    forward_across(left)
+    make_slab(right, 2)
+    forward_across(right)
     take_across(2)
     take_across(3)
-    wait_bytes(gathered.at[:, :, 1 - c], d_recv)
-    wait_bytes(scales.at[pl.ds(0, 7)], scale_sem.at[1])
-
-    @pl.loop(0, 4)
-    def _(from_x):
-        for from_c in range(2):
-            for from_z in range(4):
-                dp = from_x * 2 + from_z % 2
-                rows = pl.ds(pl.multiple_of(dp * 128, 128), 128)
-                block = gathered[from_x, from_z, 1, x] if from_c else gathered[from_x, x, 0, from_z]
-                block = (block.astype(F32) * scales[dp][:1]).astype(BF16)
-                slab[(from_z // 2) * 2 + from_c, rows, :] = jnp.transpose(block)
-
-    wait_bytes(arrived.at[0], wave_recv.at[0])
-    for half in range(2):
-        sent[0, half] = forward(0, half).astype(BF16)
-        pass_copy(half).start()
     wait_bytes(arrived.at[1], wave_recv.at[1])
-    sent[1, 1] = forward(1, 1).astype(BF16)
-    partial_copy(1, 1).start()
-    wait_bytes(arrived.at[2], wave_recv.at[2])
-    sent[2, 0] = forward(2, 0).astype(BF16)
-    partial_copy(2, 0).start()
-    held[0] = forward(1, 0)
-    held[1] = forward(2, 1)
+    forward_beside(1, x)
+    forward_beside(1, left)
+    forward_beside(1, right)
+    make_slab(across, 3)
+    forward_across(across)
+    forward_beside(1, across)
     wait_bytes(gathered.at[0, 0, 0, pl.ds(0, 3)], a_send)
     wait_bytes(gathered.at[0, pl.ds(0, 3), 0], b_send)
     wait_bytes(gathered.at[0], x_send)
     wait_bytes(gathered.at[0, pl.ds(0, 2)], f_send)
     wait_bytes(gathered.at[pl.ds(0, 2)], d_send)
-    normalise(0)
-    normalise(1)
-    pass_copy(0).wait_recv()
-    sent[1, 0] = (held[0] + passing[0].astype(F32)).astype(BF16)
-    partial_copy(1, 0).start()
-    pass_copy(1).wait_recv()
-    sent[2, 1] = (held[1] + passing[1].astype(F32)).astype(BF16)
-    partial_copy(2, 1).start()
-    normalise(2)
-    normalise(3)
+
+    @pl.loop(0, 4)
+    def _(q):
+        pass_copy(q).wait_recv()
+        add_passing(1, q)
+        normalise(q)
+
+    wait_bytes(arrived.at[2], wave_recv.at[2])
+
+    @pl.loop(0, 4)
+    def _(q):
+        forward_beside(2, q)
+        add_passing(2, q)
+
     wait_bytes(arrived.at[3], wave_recv.at[3])
     for half in range(2):
-        sums[half] = forward(3, half)
-
-    for w, half in ((1, 1), (2, 0), (1, 0), (2, 1)):
-        partial_copy(w, half).wait_recv()
-
-    for half in range(2):
-        @pl.loop(0, 2)
-        def _(part):
-            rows = pl.ds(pl.multiple_of(part * 256, 256), 256)
-            total = sums[half, rows, :] + (got[0, half, rows, :].astype(F32) + got[1, half, rows, :].astype(F32))
-            to = pl.ds(pl.multiple_of(half * 512 + part * 256, 256), 256)
-            gate_term, up_term = hidden_terms(total, adjoint[to, :])
-            terms[to, :128] = gate_term
-            terms[to, 128:] = up_term
-
-    for half in range(2):
-        pass_copy(half).wait_send()
-        for w in (1, 2):
-            partial_copy(w, half).wait_send()
+        rows = pl.ds(half * 512, 512)
+        sums[rows, :] = forward(3, rows)
+
+    load_adjoint.wait()
+
+    @pl.loop(0, 4)
+    def _(q):
+        wait_bytes(got.at[0, :, pl.ds(0, 2)], p_recv.at[q])
+        total = sums[quarter(q), :]
+        for way in range(2):
+            total = total + jnp.concatenate([got[0, way, q], got[1, way, q]], axis=1).astype(F32)
+        gate_term, up_term = hidden_terms(total, held_adjoint[quarter(q), :])
+        terms[quarter(q), :128] = gate_term
+        terms[quarter(q), 128:] = up_term
+
+    for q in range(4):
+        pass_copy(q).wait_send()
+    wait_bytes(part, p_send)
     for w in range(4):
         wait_bytes(packed.at[w, pl.ds(0, 15)], wave_send.at[w])
     for w in (2, 3):
@@ -359,9 +405,11 @@
             pltpu.VMEM((4, 4, 2, 4, 512, 128), BF16),
             pltpu.VMEM((1024, 256), BF16),
         ),
-        in_specs=[pl.BlockSpec(memory_space=pltpu.VMEM)] * 2 + [pl.BlockSpec(memory_space=pl.ANY)] * 4,
+        in_specs=[pl.BlockSpec(memory_space=pl.ANY)] * 6,
         out_specs=(pl.BlockSpec(memory_space=pltpu.VMEM),) * 2,
         scratch_shapes=[
+            pltpu.VMEM((128, 512), BF16),
+            pltpu.VMEM((1024, 128), BF16),
             pltpu.VMEM((2, 4, 64, 4096), BF16),
             pltpu.VMEM((2, 16, 4, 64, 128), BF16),
             pltpu.VMEM((4, 16, 4, 128, 128), BF16),
@@ -369,14 +417,15 @@
             pltpu.VMEM((16, 8, 128), F32),
             pltpu.VMEM((8, 8, 128), F32),
             pltpu.VMEM((4, 1024, 512), BF16),
-            pltpu.VMEM((2, 512, 512), F32),
-            pltpu.VMEM((2, 512, 512), F32),
-            pltpu.VMEM((3, 2, 512, 512), BF16),
-            pltpu.VMEM((2, 512, 512), BF16),
-            pltpu.VMEM((2, 2, 512, 512), BF16),
-            dma((2, 4)), dma((2,)), dma((4,)), dma((4,)), dma((4,)), dma((2,)), dma((2,)),
-            dma, dma((3,)), dma, dma((3,)), dma, dma((4,)), dma((4,)), dma, dma((4,)), dma((4,)), dma, dma,
-            dma((2,)), dma((2,)), dma((2, 2)), dma((2, 2)),
+            pltpu.VMEM((1024, 512), F32),
+            pltpu.VMEM((2, 4, 256, 256), F32),
+            pltpu.VMEM((4, 256, 512), BF16),
+            pltpu.VMEM((4, 256, 512), BF16),
+            pltpu.VMEM((2, 2, 4, 256, 256), BF16),
+            pltpu.VMEM((2, 2, 4, 256, 256), BF16),
+            dma((2,)), dma((2, 4)), dma((2,)), dma((4,)), dma((4,)), dma((4,)), dma((2,)), dma((2,)),
+            dma, dma((3,)), dma, dma((3, 4)), dma, dma((4,)), dma((4,)), dma, dma((4,)), dma((4,)), dma, dma((4,)),
+            dma((4,)), dma((4,)), dma, dma((4,)),
         ],
         compiler_params=pltpu.CompilerParams(
             collective_id=0, has_side_effects=True, vmem_limit_bytes=44 * 2**20

time: 135 us -> 129 us (0.956)
  Pallas kernels: 134 us -> 129 us
    pallas_call x1, Pallas kernels: 128 us -> 123 us  [local(): pl.pallas_call(exchange, out_shape=(pltpu.VMEM((4, 4, 2, 4, 512, 128), BF...]
where the time goes in v5:
time: 129 us
  Pallas kernels  129 us (100%)
    pallas_call x1, Pallas kernels, local(): pl.pallas_call(exchange, out_shape=(pltpu.VMEM((4, 4, 2, 4, 512, 128), BF...  123 us
    pallas_call x1, Pallas kernels, local(): pl.pallas_call(product, out_shape=(jax.ShapeDtypeStruct((8192, 128), F32)...  6.03 us

profile of v5, /device:TPU:1, one launch (start us, length us, event | category | flops | bytes accessed | tf_op | source)
XLA Modules:
  0.0 129.3 jit_solution(7283270434867577669)
XLA Ops:
  0.6 122.7 %exchange.1 = (bf16[4,4,2,4,512,128]{5,4,3,2,1,0:T(8,128)(2,1)S(1)}, bf16[1024,256]{1,0:T(8,128)(2,1)S(1)}) custom-call(bf16[128,512]{1,0:T(8,128)(2,1)} %tokens.1, bf16[1024,128]{1,0:T(8,128)(2,1)} %adjoint.1, bf16[64,16384]{1,0:T(8,128)(2,1)} %w0.1, bf16[64,16384]{1,0:T(8,128)(2,1)} %w1.1, bf16[64,16384]{1,0:T(8,128)(2,1)} %w2.1, bf16[64,16384]{1,0:T(8,128)(2,1)} %w3.1), custom_call_target="tpu_custom_call" | custom-call | tf_op jit(solution)/shard_map/exchange/pallas_call | solution.py:402
  123.3 6.0 %product.1 = (f32[8192,128]{1,0:T(8,128)}, f32[8192,128]{1,0:T(8,128)}) custom-call(bf16[4,4,2,4,512,128]{5,4,3,2,1,0:T(8,128)(2,1)S(1)} %get-tuple-element.4.gathered, bf16[1024,256]{1,0:T(8,128)(2,1)S(1)} %get-tuple-element.5.terms), custom_call_target="tpu_custom_call" | custom-call | tf_op jit(solution)/shard_map/product/pallas_call | solution.py:438

commit v6 on v5

--- a/solution.py
+++ b/solution.py
@@ -107,20 +107,24 @@
         if w + 2 < 4:
             stage(w + 2)
 
-    def send_wave(w):
-        their_copy(w).wait_recv()
+    def send_wave(w, slots=(0, 4), sem=None):
+        slots, sem = pl.ds(slots[0], slots[1]), w if sem is None else sem
+        if sem == w:
+            their_copy(w).wait_recv()
         for dy, dz in PLANE:
             to_y = (y + dy * (1 - c) + (4 - dz) * c) % 4
             to_z = (z + dz * (1 - c) + (4 - dy) * c) % 4
             pltpu.make_async_remote_copy(
-                packed.at[w, chip_in_plane(to_y, to_z)],
-                arrived.at[w, me],
+                packed.at[w, chip_in_plane(to_y, to_z), slots],
+                arrived.at[w, me, slots],
                 wave_send.at[w],
-                wave_recv.at[w],
+                wave_recv.at[sem],
                 device(x, to_y, to_z, c),
                 MESH,
             ).start()
-        pltpu.make_async_copy(packed.at[w, me], arrived.at[w, me], wave_recv.at[w]).start()
+        pltpu.make_async_copy(
+            packed.at[w, me, slots], arrived.at[w, me, slots], wave_recv.at[sem]
+        ).start()
 
     def wait_bytes(ref, sem):
         pltpu.make_async_copy(ref, ref, sem).wait()
@@ -178,9 +182,9 @@
         wait_bytes(gathered.at[across, pl.ds(2, 2), c, column_b[i]], f_right.at[i])
         share(gathered.at[across, :, c, column_b[i]], 3)
 
-    def forward(w, rows):
+    def forward(w, rows, slots=range(4)):
         lhs = jnp.concatenate([slab[k, rows, :] for k in range(4)], axis=1)
-        rhs = jnp.concatenate([arrived[w, :, m].reshape(2048, 128) for m in range(4)], axis=1)
+        rhs = jnp.concatenate([arrived[w, :, m].reshape(2048, 128) for m in slots], axis=1)
         return jnp.dot(lhs, rhs, preferred_element_type=F32)
 
     def quarter(q):
@@ -303,7 +307,8 @@
     make_slab(x, 0)
     pass_on(1)
     take_across(0)
-    send_wave(3)
+    send_wave(3, (0, 2))
+    send_wave(3, (2, 2), 4)
     wait_bytes(arrived.at[0], wave_recv.at[0])
     forward_across(x)
     pass_on(2)
@@ -322,6 +327,18 @@
     make_slab(across, 3)
     forward_across(across)
     forward_beside(1, across)
+    @pl.loop(0, 4)
+    def _(q):
+        pass_copy(q).wait_recv()
+        add_passing(1, q)
+
+    wait_bytes(arrived.at[2], wave_recv.at[2])
+
+    @pl.loop(0, 4)
+    def _(q):
+        forward_beside(2, q)
+        add_passing(2, q)
+
     wait_bytes(gathered.at[0, 0, 0, pl.ds(0, 3)], a_send)
     wait_bytes(gathered.at[0, pl.ds(0, 3), 0], b_send)
     wait_bytes(gathered.at[0], x_send)
@@ -330,21 +347,13 @@
 
     @pl.loop(0, 4)
     def _(q):
-        pass_copy(q).wait_recv()
-        add_passing(1, q)
         normalise(q)
 
-    wait_bytes(arrived.at[2], wave_recv.at[2])
-
-    @pl.loop(0, 4)
-    def _(q):
-        forward_beside(2, q)
-        add_passing(2, q)
-
-    wait_bytes(arrived.at[3], wave_recv.at[3])
-    for half in range(2):
-        rows = pl.ds(half * 512, 512)
-        sums[rows, :] = forward(3, rows)
+    for pair in range(2):
+        wait_bytes(arrived.at[3, :, pl.ds(pair * 2, 2)], wave_recv.at[3 + pair])
+        for half in range(2):
+            rows = pl.ds(half * 512, 512)
+            sums[rows, pair * 256 : pair * 256 + 256] = forward(3, rows, (pair * 2, pair * 2 + 1))
 
     load_adjoint.wait()
 
@@ -423,7 +432,7 @@
             pltpu.VMEM((4, 256, 512), BF16),
             pltpu.VMEM((2, 2, 4, 256, 256), BF16),
             pltpu.VMEM((2, 2, 4, 256, 256), BF16),
-            dma((2,)), dma((2, 4)), dma((2,)), dma((4,)), dma((4,)), dma((4,)), dma((2,)), dma((2,)),
+            dma((2,)), dma((2, 4)), dma((2,)), dma((4,)), dma((4,)), dma((5,)), dma((2,)), dma((2,)),
             dma, dma((3,)), dma, dma((3, 4)), dma, dma((4,)), dma((4,)), dma, dma((4,)), dma((4,)), dma, dma((4,)),
             dma((4,)), dma((4,)), dma, dma((4,)),
         ],

time: 129 us -> 128 us (level)
  Pallas kernels: 129 us -> 127 us
    pallas_call x1, Pallas kernels: 123 us -> 121 us  [local(): pl.pallas_call(exchange, out_shape=(pltpu.VMEM((4, 4, 2, 4, 512, 128), BF...]
where the time goes in v6:
time: 128 us
  Pallas kernels  127 us (99%)
    pallas_call x1, Pallas kernels, local(): pl.pallas_call(exchange, out_shape=(pltpu.VMEM((4, 4, 2, 4, 512, 128), BF...  121 us
    pallas_call x1, Pallas kernels, local(): pl.pallas_call(product, out_shape=(jax.ShapeDtypeStruct((8192, 128), F32)...  6.03 us

profile of v6, /device:TPU:1, one launch (start us, length us, event | category | flops | bytes accessed | tf_op | source)
XLA Modules:
  0.0 127.6 jit_solution(7972629165070191747)
XLA Ops:
  0.6 120.9 %exchange.1 = (bf16[4,4,2,4,512,128]{5,4,3,2,1,0:T(8,128)(2,1)S(1)}, bf16[1024,256]{1,0:T(8,128)(2,1)S(1)}) custom-call(bf16[128,512]{1,0:T(8,128)(2,1)} %tokens.1, bf16[1024,128]{1,0:T(8,128)(2,1)} %adjoint.1, bf16[64,16384]{1,0:T(8,128)(2,1)} %w0.1, bf16[64,16384]{1,0:T(8,128)(2,1)} %w1.1, bf16[64,16384]{1,0:T(8,128)(2,1)} %w2.1, bf16[64,16384]{1,0:T(8,128)(2,1)} %w3.1), custom_call_target="tpu_custom_call" | custom-call | tf_op jit(solution)/shard_map/exchange/pallas_call | solution.py:411
  121.5 6.0 %product.1 = (f32[8192,128]{1,0:T(8,128)}, f32[8192,128]{1,0:T(8,128)}) custom-call(bf16[4,4,2,4,512,128]{5,4,3,2,1,0:T(8,128)(2,1)S(1)} %get-tuple-element.4.gathered, bf16[1024,256]{1,0:T(8,128)(2,1)S(1)} %get-tuple-element.5.terms), custom_call_target="tpu_custom_call" | custom-call | tf_op jit(solution)/shard_map/product/pallas_call | solution.py:447

commit v7 on v6

--- a/solution.py
+++ b/solution.py
@@ -262,6 +262,16 @@
             mine, mine, a_send, a_recv.at[i], at_ab((a + d) % 4, b), MESH
         ).start()
     send_block(0)
+    send_block(1)
+    send_block(2)
+    pack(0)
+    their_copy(0).start()
+    relay_block(1, 0)
+    relay_block(2, 0)
+    send_block(3)
+    relay_block(3, 0)
+    share(gathered.at[x, :, c, b], 0)
+    send_wave(0)
     wide = turned.astype(F32)
     t = lax.axis_index("tensor")
     stats[t] = jnp.broadcast_to(jnp.sum(wide * wide, axis=0, keepdims=True), (8, 128))
@@ -269,18 +279,16 @@
         pltpu.make_async_remote_copy(
             stats.at[t], stats.at[t], stat_sem.at[0], stat_sem.at[1], peer, MESH
         ).start()
-    pack(0)
-    their_copy(0).start()
-    send_block(1)
-    send_block(2)
-    relay_block(1, 0)
-    relay_block(2, 0)
-    send_block(3)
-    relay_block(3, 0)
-    share(gathered.at[x, :, c, b], 0)
-    send_wave(0)
     pack(1)
     their_copy(1).start()
+    for k in (1, 2, 3):
+        for i in (1, 2, 3):
+            relay_block(i, k)
+    for i in (1, 2, 3):
+        share(gathered.at[x, :, c, column_b[i]], 0)
+    send_wave(1)
+    pack(2)
+    their_copy(2).start()
     wait_bytes(stats.at[pl.ds(0, 15)], stat_sem.at[1])
     total = stats[0]
     for i in range(1, 16):
@@ -291,24 +299,16 @@
         pltpu.make_async_remote_copy(
             scales.at[dp], scales.at[dp], scale_sem.at[0], scale_sem.at[1], peer, MESH
         ).start()
-    for k in (1, 2, 3):
-        for i in (1, 2, 3):
-            relay_block(i, k)
-    for i in (1, 2, 3):
-        share(gathered.at[x, :, c, column_b[i]], 0)
-    send_wave(1)
-    pack(2)
-    their_copy(2).start()
     pass_on(0)
     send_wave(2)
     pack(3)
     their_copy(3).start()
-    wait_bytes(scales.at[pl.ds(0, 7)], scale_sem.at[1])
-    make_slab(x, 0)
     pass_on(1)
     take_across(0)
     send_wave(3, (0, 2))
     send_wave(3, (2, 2), 4)
+    wait_bytes(scales.at[pl.ds(0, 7)], scale_sem.at[1])
+    make_slab(x, 0)
     wait_bytes(arrived.at[0], wave_recv.at[0])
     forward_across(x)
     pass_on(2)

time: 128 us -> 128 us (level)
  no operation moved by 1% of the time
where the time goes in v7:
time: 128 us
  Pallas kernels  127 us (99%)
    pallas_call x1, Pallas kernels, local(): pl.pallas_call(exchange, out_shape=(pltpu.VMEM((4, 4, 2, 4, 512, 128), BF...  121 us
    pallas_call x1, Pallas kernels, local(): pl.pallas_call(product, out_shape=(jax.ShapeDtypeStruct((8192, 128), F32)...  6.03 us

profile of v7, /device:TPU:1, one launch (start us, length us, event | category | flops | bytes accessed | tf_op | source)
XLA Modules:
  0.0 127.7 jit_solution(4011947637267325166)
XLA Ops:
  0.6 121.1 %exchange.1 = (bf16[4,4,2,4,512,128]{5,4,3,2,1,0:T(8,128)(2,1)S(1)}, bf16[1024,256]{1,0:T(8,128)(2,1)S(1)}) custom-call(bf16[128,512]{1,0:T(8,128)(2,1)} %tokens.1, bf16[1024,128]{1,0:T(8,128)(2,1)} %adjoint.1, bf16[64,16384]{1,0:T(8,128)(2,1)} %w0.1, bf16[64,16384]{1,0:T(8,128)(2,1)} %w1.1, bf16[64,16384]{1,0:T(8,128)(2,1)} %w2.1, bf16[64,16384]{1,0:T(8,128)(2,1)} %w3.1), custom_call_target="tpu_custom_call" | custom-call | tf_op jit(solution)/shard_map/exchange/pallas_call | solution.py:411
  121.7 6.0 %product.1 = (f32[8192,128]{1,0:T(8,128)}, f32[8192,128]{1,0:T(8,128)}) custom-call(bf16[4,4,2,4,512,128]{5,4,3,2,1,0:T(8,128)(2,1)S(1)} %get-tuple-element.4.gathered, bf16[1024,256]{1,0:T(8,128)(2,1)S(1)} %get-tuple-element.5.terms), custom_call_target="tpu_custom_call" | custom-call | tf_op jit(solution)/shard_map/product/pallas_call | solution.py:447
